TPU v7x, 256 devices: a whole 4x4x8 slice. The times are simulated.
256 devices in a mesh: section: 4 (over y), dp: 16 (over z_hi, x), tensor: 4 (over z_lo, core).
Axes of the slice: x: 4, y: 4, z: 8 (z_hi: 4, z_lo: 2; z = z_hi * 2 + z_lo), core: 2. Of those that a mesh axis runs over, the one named last changes fastest.
Arguments:
- states: bfloat16 [32, 128, 8192], P('dp', None, ('section', 'tensor')), may hold values from -60 to 60
- gain: bfloat16 [8192], P(('section', 'tensor')), may hold values from 0.25 to 1.75
- kv_weight: bfloat16 [4, 8192, 2, 2048], P('section', 'dp', None, 'tensor'), may hold values from -0.0625 to 0.0625
- queries: bfloat16 [4, 32, 256, 2048], P('section', 'dp', None, 'tensor'), may hold values from -6 to 6
- out_grad: bfloat16 [4, 32, 256, 2048], P('section', 'dp', None, 'tensor'), may hold values from -24 to 24
- src_len: int32 [32], P('dp'), may hold values from 32 to 128, as said below
Outputs:
- attended: bfloat16 [4, 32, 256, 2048], P('section', 'dp', None, 'tensor')
- grad_queries: bfloat16 [4, 32, 256, 2048], P('section', 'dp', None, 'tensor')
- grad_states: float32 [32, 128, 8192], P('dp', None, ('section', 'tensor'))
- grad_gain: float32 [8192], P(('section', 'tensor'))
Inputs may be any that keep to these rules, and one draw needn't show every extreme that they name: `src_len`: the largest value 128 is reached.
All inputs are finite; a program needn't handle non-finite values.
Results may differ from a plain program's by a relative error of at most 0.0095.
Values may be sent and summed in bfloat16 or wider, within the bound.
A program may use at most 128 MiB of HBM per device.

v0:
```python
import jax
import jax.numpy as jnp
from jax import lax
from jax.sharding import PartitionSpec as P

HEAD_DIM = 64


def per_device(states, gain, kv_weight, queries, out_grad, src_len):
    batch_local = states.shape[0]
    src_rows = states.shape[1]
    head_cols = queries.shape[-1]
    heads_local = head_cols // HEAD_DIM
    tgt_rows = queries.shape[2]
    scale = HEAD_DIM ** (-0.5)
    weights = lax.all_gather(kv_weight, "dp", axis=1, tiled=True)[0]
    full_states, full_gain = (
        lax.all_gather(states, ("section", "tensor"), axis=2, tiled=True),
        lax.all_gather(gain, ("section", "tensor"), axis=0, tiled=True),
    )
    hf = full_states.astype(jnp.float32)
    gf = full_gain.astype(jnp.float32)
    inv = 1.0 / jnp.sqrt(jnp.mean(hf * hf, axis=-1) + 1e-06)
    normed = (hf * inv[..., None] * gf).astype(jnp.bfloat16)
    kv = jnp.einsum("bsd,dch->bsch", normed, weights, preferred_element_type=jnp.float32).astype(
        jnp.bfloat16
    )
    keys = kv[:, :, 0].reshape(batch_local, src_rows, heads_local, HEAD_DIM)
    values = kv[:, :, 1].reshape(batch_local, src_rows, heads_local, HEAD_DIM)
    query = queries[0].reshape(batch_local, tgt_rows, heads_local, HEAD_DIM)
    cotan = out_grad[0].reshape(batch_local, tgt_rows, heads_local, HEAD_DIM)
    valid = jnp.arange(src_rows, dtype=jnp.int32)[None, :] < src_len[:, None]
    scores = jnp.einsum("bthe,bshe->bhts", query, keys, preferred_element_type=jnp.float32) * scale
    expo = jnp.where(valid[:, None, None, :], jnp.exp(scores), 0.0)
    probs = expo / jnp.sum(expo, axis=-1, keepdims=True)
    probs_b = probs.astype(jnp.bfloat16)
    attended = jnp.einsum(
        "bhts,bshe->bthe", probs_b, values, preferred_element_type=jnp.float32
    ).astype(jnp.bfloat16)
    dprob = jnp.einsum("bthe,bshe->bhts", cotan, values, preferred_element_type=jnp.float32)
    delta = jnp.sum(probs * dprob, axis=-1, keepdims=True)
    dscore = (probs * (dprob - delta) * scale).astype(jnp.bfloat16)
    grad_q = jnp.einsum("bhts,bshe->bthe", dscore, keys, preferred_element_type=jnp.float32).astype(
        jnp.bfloat16
    )
    dkey = jnp.einsum("bhts,bthe->bshe", dscore, query, preferred_element_type=jnp.float32).astype(
        jnp.bfloat16
    )
    dvalue = jnp.einsum(
        "bhts,bthe->bshe", probs_b, cotan, preferred_element_type=jnp.float32
    ).astype(jnp.bfloat16)
    dkv = jnp.stack(
        [
            dkey.reshape(batch_local, src_rows, head_cols),
            dvalue.reshape(batch_local, src_rows, head_cols),
        ],
        axis=2,
    )
    term = jnp.einsum("bsch,dch->bsd", dkv, weights, preferred_element_type=jnp.float32)
    dnormed = lax.psum_scatter(term, ("section", "tensor"), scatter_dimension=2, tiled=True)
    own_states = states.astype(jnp.float32)
    own_gain = gain.astype(jnp.float32)
    rowdot = lax.psum(jnp.sum(dnormed * own_states * own_gain, axis=-1), ("section", "tensor"))
    total_width = full_states.shape[2]
    grad_states = (
        own_gain * inv[..., None] * dnormed
        - own_states * (rowdot * inv * inv * inv)[..., None] / total_width
    )
    gain_term = jnp.sum(dnormed * own_states * inv[..., None], axis=(0, 1))
    grad_gain = lax.psum(gain_term, "dp")
    attended_out = attended.reshape(1, batch_local, tgt_rows, head_cols)
    grad_q_out = grad_q.reshape(1, batch_local, tgt_rows, head_cols)
    return (attended_out, grad_q_out, grad_states, grad_gain)


def solution(mesh):
    return jax.shard_map(
        per_device,
        mesh=mesh,
        in_specs=(
            P("dp", None, ("section", "tensor")),
            P(("section", "tensor")),
            P("section", "dp", None, "tensor"),
            P("section", "dp", None, "tensor"),
            P("section", "dp", None, "tensor"),
            P("dp"),
        ),
        out_specs=(
            P("section", "dp", None, "tensor"),
            P("section", "dp", None, "tensor"),
            P("dp", None, ("section", "tensor")),
            P(("section", "tensor")),
        ),
        check_vma=False,
    )
```

profile of v0, /device:TPU:1, one launch (start us, length us, event | category | flops | bytes accessed | tf_op | source)
XLA Modules:
  0.0 471.4 jit_solution(2857464814548965880)
XLA Ops:
  7.2 0.0 copy-start.5
  7.2 0.0 copy-start.1
  7.2 0.0 all-gather.4.cloned.1.call-start
  7.2 0.7 all-gather.4.cloned.1.call-update
  7.9 0.0 copy-start.2
  7.9 0.0 all-gather.6.cloned.1.call-start
  8.0 2.4 copy.40
  10.4 0.0 copy-start.6
  10.4 0.0 all-gather.6.cloned.1.call-update
  10.4 0.0 reduce-scatter.2.cloned.1.call-start
  10.5 0.0 copy-done.5
  10.5 21.7 %all-gather = bf16[16,1,512]{2,1,0:T(2,128)(2,1)S(1)} all-gather(bf16[1,1,512]{2,1,0:T(2,128)(2,1)S(1)} %reshape.43), channel_id=1, replica_groups=mesh['section'=4,'dp'=16,'tensor'=4] {'section','tensor'}, dimensions={0}, use_global_device_ids=true | all-gather | bytes 17408 | tf_op jit(solution)/shard_map/all_gather | solution.py:19
  32.3 0.0 copy-done.1
  32.3 0.2 copy.43
  32.5 0.0 copy-done.2
  32.5 0.2 copy.45
  32.7 0.0 copy-done.6
  32.7 0.1 iota_compare_fusion
  32.8 21.2 %all-gather.4.cloned.1.call-done = bf16[2,128,8192]{2,1,0:T(8,128)(2,1)} async-done(((bf16[2,128,512]{2,1,0:T(8,128)(2,1)}), bf16[2,128,8192]{2,1,0:T(8,128)(2,1)}) %all-gather.4.cloned.1.call-update) | async-done | bytes 4194320 | tf_op jit(solution)/shard_map/all_gather | solution.py:18
  54.0 3.1 fusion.8
  57.1 200.5 %all-gather.6.cloned.1.call-done = bf16[1,8192,2,512]{3,1,2,0:T(8,128)(2,1)} async-done(((bf16[1,512,2,512]{3,1,2,0:T(8,128)(2,1)}), bf16[1,8192,2,512]{3,1,2,0:T(8,128)(2,1)}) %all-gather.6.cloned.1.call-update) | async-done | bytes 16777232 | tf_op jit(solution)/shard_map/all_gather | solution.py:16
  257.6 11.6 %fusion.18 = bf16[2,128,2,512]{3,1,2,0:T(8,128)(2,1)S(1)} fusion(bf16[1,8192,2,512]{3,1,2,0:T(8,128)(2,1)} %all-gather.6.cloned.1.call-done, bf16[2,128,8192]{2,1,0:T(8,128)(2,1)} %all-gather.4.cloned.1.call-done, f32[8192]{0:T(1024)S(1)} %bitcast.101, f32[2,128]{1,0:T(2,128)S(1)} %add_rsqrt_fusion), kind=kOutput, calls=%fused_computation.24 | convolution fusion | flops 4303618048 | bytes 21529600 | tf_op jit(solution)/shard_map/bsd,dch->bsch/dot_general | solution.py:25
  269.2 0.2 copy.41
  269.4 0.8 copy.42
  270.3 0.0 copy-start.3
  270.3 0.5 fusion.37
  270.8 0.5 copy-done.3
  271.2 0.6 bitcast_reduce_fusion
  271.9 0.0 copy-start.7
  271.9 1.4 convolution_convert_fusion.2
  273.3 0.0 copy-done.7
  273.3 1.1 copy.50
  274.4 3.6 convolution_convert_fusion.3
  278.0 0.1 copy.49
  278.1 18.8 %fusion.5 = f32[2,128,8192]{2,1,0:T(8,128)} fusion(bf16[1,8192,2,512]{3,1,2,0:T(8,128)(2,1)} %all-gather.6.cloned.1.call-done, bf16[2,128,1,512]{3,1,2,0:T(8,128)(2,1)S(1)} %copy.50, bf16[2,128,1,512]{3,1,2,0:T(8,128)(2,1)S(1)} %copy.49), kind=kOutput, calls=%fused_computation.5 | convolution fusion | flops 4295229440 | bytes 25690112 | tf_op jit(solution)/shard_map/bsch,dch->bsd/dot_general | solution.py:59
  297.0 0.0 reduce-scatter.2.cloned.1.call-update
  297.0 0.0 copy-start.4
  297.0 2.3 convolution_convert_fusion.1
  299.3 1.0 copy.51
  300.3 0.0 copy-done.4
  300.3 0.0 copy-start
  300.3 3.6 convolution_convert_fusion
  303.9 1.0 copy.52
  304.9 90.2 %reduce-scatter.2.cloned.1.call-done = f32[2,128,512]{2,1,0:T(8,128)} async-done(((f32[2,128,8192]{2,1,0:T(8,128)}), f32[2,128,512]{2,1,0:T(8,128)}) %reduce-scatter.2.cloned.1.call-update) | async-done | bytes 524304 | tf_op jit(solution)/shard_map/reduce_scatter | solution.py:60
  395.1 0.0 copy-done
  395.1 1.2 multiply_reduce_fusion
  396.3 28.9 %psum.14 = f32[2,128]{1,0:T(2,128)S(1)} all-reduce(f32[2,128]{1,0:T(2,128)S(1)} %get-tuple-element.17), channel_id=1, replica_groups=mesh['section'=4,'dp'=16,'tensor'=4] {'section','tensor'}, use_global_device_ids=true, to_apply=%region_5.6 | all-reduce | flops 256 | bytes 2048 | tf_op jit(solution)/shard_map/psum | solution.py:63
  425.2 37.7 %psum.15 = f32[512]{0:T(512)} all-reduce(f32[512]{0:T(512)S(1)} %get-tuple-element.16), channel_id=1, replica_groups=mesh['section'=4,'dp'=16,'tensor'=4] {'dp'}, use_global_device_ids=true, to_apply=%region_7.8 | all-reduce | flops 512 | bytes 4096 | tf_op jit(solution)/shard_map/psum | solution.py:70
  462.9 2.0 fusion.25
  (6 shorter events, 0.1 us)
Async XLA Ops:
  7.2 3.3 copy-start.5
  7.2 25.1 %copy-start.1 = (bf16[1,2,256,512]{3,2,1,0:T(8,128)(2,1)S(1)}, bf16[1,2,256,512]{3,2,1,0:T(8,128)(2,1)}, u32[]{:S(2)}) copy-start(bf16[1,2,256,512]{3,2,1,0:T(8,128)(2,1)} %param.9) | copy-start | bytes 1572868
  7.2 46.8 %all-gather.4.cloned.1.call-start = ((), (), s32[]{:S(2)}) async-start(), calls=%async_computation.1 | async-start | bytes 4456448 | tf_op jit(solution)/shard_map/all_gather | solution.py:18
  7.9 24.6 %copy-start.2 = (bf16[1,2,256,512]{3,2,1,0:T(8,128)(2,1)S(1)}, bf16[1,2,256,512]{3,2,1,0:T(8,128)(2,1)}, u32[]{:S(2)}) copy-start(bf16[1,2,256,512]{3,2,1,0:T(8,128)(2,1)} %param.10) | copy-start | bytes 1572868
  7.9 249.7 %all-gather.6.cloned.1.call-start = ((), (), s32[]{:S(2)}) async-start(), calls=%async_computation.2 | async-start | bytes 17825792 | tf_op jit(solution)/shard_map/all_gather | solution.py:16
  10.4 22.3 %copy-start.6 = (s32[2]{0:T(128)S(1)}, s32[2]{0:T(128)}, u32[]{:S(2)}) copy-start(s32[2]{0:T(128)} %param.11) | copy-start | bytes 28
  10.4 384.7 %reduce-scatter.2.cloned.1.call-start = ((), (), s32[]{:S(2)}) async-start(), calls=%async_computation.3 | async-start | bytes 8912896 | tf_op jit(solution)/shard_map/reduce_scatter | solution.py:60
  270.3 0.9 copy-start.3
  271.9 1.4 copy-start.7
  297.0 3.3 copy-start.4
  300.3 94.8 %copy-start = (bf16[2,128,512]{2,1,0:T(8,128)(2,1)S(1)}, bf16[2,128,512]{2,1,0:T(8,128)(2,1)}, u32[]{:S(2)}) copy-start(bf16[2,128,512]{2,1,0:T(8,128)(2,1)} %param.6) | copy-start | bytes 786436
Sparse Core Ops, SparseCore 0:
  9.8 44.1 all-gather.3
  56.5 201.1 all-gather.5
  297.1 97.9 reduce-scatter.1
where the time goes:
time: 477 us; the launch traced here: 471 us
  waiting for transfers between devices  313 us (66%)
  blocking collectives  88.3 us (19%)
  matrix products  42.4 us (9%)
  between operations  13.9 us (3%)
  local copies, waits for them, and re-layouts  7.62 us (2%)
  other arithmetic  6.44 us (1%)
    all_gather x1, waiting for transfers between devices, per_device(): weights = lax.all_gather(kv_weight, 'dp', axis=1, tiled=True)[0]  200 us
    reduce_scatter x1, waiting for transfers between devices, per_device(): lax.psum_scatter(term, ('section', 'tensor'), scatter_dimension=2, tiled=...  90.2 us
    psum x1, blocking collectives, per_device(): grad_gain = lax.psum(gain_term, 'dp')  37.7 us
    psum x1, blocking collectives, per_device(): lax.psum(jnp.sum(dnormed * own_states * own_gain, axis=-1), ('section', '...  28.9 us
    all_gather x1, blocking collectives, per_device(): lax.all_gather(gain, ('section', 'tensor'), axis=0, tiled=True)  21.7 us
    all_gather x1, waiting for transfers between devices, per_device(): lax.all_gather(states, ('section', 'tensor'), axis=2, tiled=True)  21.2 us
    dot_general x1, matrix products, per_device(): jnp.einsum('bsch,dch->bsd', dkv, weights, preferred_element_type=jnp.floa...  18.8 us
    dot_general x1, matrix products, per_device(): jnp.einsum('bsd,dch->bsch', normed, weights, preferred_element_type=jnp.f...  11.6 us
  transfers between devices with their start and end apart: 3, of which 3 were waited for; matrix products, arithmetic and copies ran while one was open for 3% of the time, Pallas kernels for 0%

commit v1 on v0

v1 whole, which is shorter than its diff:
```python
import jax
import jax.numpy as jnp
from jax import lax
from jax.experimental import pallas as pl
from jax.experimental.pallas import tpu as pltpu
from jax.sharding import PartitionSpec as P

MESH = pl.DeviceIdType.MESH
HEAD_DIM = 64
SCALE = HEAD_DIM ** (-0.5)
EPS = 1e-06
MASKED = -1e30
NX, NY, NZ = 4, 4, 4
CHUNKS = 4
F32, BF16 = jnp.float32, jnp.bfloat16


def rotate(a, by, n):
    return lax.rem(a + by, n)


def kernel(
    w_ref, states_ref, gain_ref, q_ref, og_ref, bias_ref,
    att_ref, gq_ref, gs_ref, gg_ref,
    hg, wg, a, own_part, part_send, rs_recv, ag, dn, core_send, core_recv, y_send, y_recv, y_own,
    fin_send, fin, kvf, racc, small, gsum, inv_ref, rsum_ref,
    local_sem, wd_s, wd_r, wf_s, wf_r, s1_s, s1_r, s2_s, s2_r, s3_s, s3_r, rs_s, rs_r, ag_s, ag_r,
    d1_s, d1_r, d2_s, d2_r, d3_s, d3_r, sm_s, sm_r, gs_s, gs_r,
):
    y, d, t = lax.axis_index("section"), lax.axis_index("dp"), lax.axis_index("tensor")
    zh, x, zl, core = d // 4, lax.rem(d, 4), t // 2, lax.rem(t, 2)
    rows, feats = states_ref.shape
    batches = q_ref.shape[0]
    src = rows // batches
    cols = w_ref.shape[2]

    def at(y_=None, zh_=None, x_=None, zl_=None, core_=None):
        pick = lambda new, old: old if new is None else new
        return (pick(y_, y), pick(zh_, zh) * 4 + pick(x_, x), pick(zl_, zl) * 2 + pick(core_, core))

    def copy(src_ref, dst_ref, send, recv, to):
        return pltpu.make_async_remote_copy(
            src_ref=src_ref, dst_ref=dst_ref, send_sem=send, recv_sem=recv, device_id=to, device_id_type=MESH
        )

    other = 1 - core
    home = t == x

    barrier = pltpu.get_barrier_semaphore()

    def greet(to):
        pl.semaphore_signal(barrier, inc=1, device_id=to, device_id_type=MESH)

    for k in (1, 2, 3):
        greet(at(zh_=rotate(zh, k, NZ)))
        greet(at(y_=rotate(y, k, NY)))
        greet(at(x_=rotate(x, k, NX)))
    greet(at(core_=other))
    greet(at(zl_=1 - zl))
    x_core = lax.rem(x, 2)
    greet(at(x_=t, zl_=1 - zl, core_=x_core))
    source = lambda half: (y, zh * 4 + core + 2 * half, x)
    far_half = jnp.where(home, 1 - x // 2, 0)

    @pl.when(jnp.logical_not(home))
    def _():
        greet(at(x_=t, core_=x_core))
        greet(source(0))
        greet(source(1))
        pl.semaphore_wait(barrier, 15)

    @pl.when(home)
    def _():
        greet(source(far_half))
        pl.semaphore_wait(barrier, 13)

    def w_direct(c, up):
        to = at(zh_=rotate(zh, 1 if up else 3, NZ))
        return copy(w_ref.at[c], wg.at[3 if up else 1, c], wd_s.at[int(up), c], wd_r.at[int(up), c], to)

    def w_forward(c, up):
        half = feats // 2
        part = pl.ds(0 if up else half, half)
        to = at(zh_=rotate(zh, 1 if up else 3, NZ))
        return copy(
            wg.at[3 if up else 1, c, part], wg.at[2, c, part], wf_s.at[int(up), c], wf_r.at[int(up), c], to
        )

    def pump(c):
        for up in (True, False):
            w_direct(c, up).wait_recv()
            w_forward(c, up).start()

    def w_send(c):
        for up in (True, False):
            w_direct(c, up).start()

    own_w = pltpu.make_async_copy(w_ref, wg.at[0], local_sem.at[0])
    own_w.start()
    w_send(0)

    h = states_ref[...].astype(F32)
    hg[...] = (h * gain_ref[...]).astype(BF16)
    squares = h * h

    def s1_copy(z, to):
        return copy(hg, a.at[x, y], s1_s.at[z], s1_r.at[x // 2], to)

    s1_far = s1_copy(1, at(x_=t, zl_=1 - zl, core_=x_core))
    s1_near = s1_copy(0, at(x_=t, core_=x_core))
    s1_local = pltpu.make_async_copy(hg, a.at[x, y], s1_r.at[x // 2])
    s1_far.start()

    @pl.when(jnp.logical_not(home))
    def _():
        s1_near.start()

    @pl.when(home)
    def _():
        s1_local.start()

    w_send(1)

    def total_lanes(v):
        acc = v[:, :128]
        for k in range(128, v.shape[1], 128):
            acc = acc + v[:, k : k + 128]
        return jnp.broadcast_to(jnp.sum(acc.T, axis=0, keepdims=True), (8, rows))

    def spread(row):
        return jnp.broadcast_to(row, (128, rows)).T

    def reduce_start(base, v):
        small[base] = v
        c = copy(small.at[base], small.at[base + 1], sm_s.at[base], sm_r.at[base + 1], at(core_=other))
        c.start()

    def reduce_zl(base):
        copy(small.at[base], small.at[base + 1], sm_s.at[base], sm_r.at[base + 1], at(core_=other)).wait()
        small[base + 2] = small[base] + small[base + 1]
        copy(small.at[base + 2], small.at[base + 3], sm_s.at[base + 2], sm_r.at[base + 3], at(zl_=1 - zl)).start()

    def reduce_y_copies(base):
        return [
            copy(
                small.at[base + 4], small.at[base + 4 + k], sm_s.at[base + 4 + k], sm_r.at[base + 4 + k],
                at(y_=rotate(y, k, NY)),
            )
            for k in (1, 2, 3)
        ]

    def reduce_y(base):
        copy(small.at[base + 2], small.at[base + 3], sm_s.at[base + 2], sm_r.at[base + 3], at(zl_=1 - zl)).wait()
        small[base + 4] = small[base + 2] + small[base + 3]
        for c in reduce_y_copies(base):
            c.start()

    def reduce_end(base):
        for c in reduce_y_copies(base):
            c.wait()
        return (small[base + 4] + small[base + 5]) + (small[base + 6] + small[base + 7])

    reduce_start(0, total_lanes(squares))

    def s2_copy(half, k):
        piece = a.at[core + 2 * half, y]
        return copy(piece, piece, s2_s.at[half, k - 1], s2_r.at[half, k - 1], at(y_=rotate(y, k, NY)))

    def s2_arrival(half, k):
        piece = a.at[core + 2 * half, rotate(y, 4 - k, NY)]
        return copy(piece, piece, s2_s.at[half, k - 1], s2_r.at[half, k - 1], at(y_=rotate(y, k, NY)))

    def s3_copy(half, k):
        piece = a.at[core + 2 * half, rotate(y, 4 - k, NY)]
        return copy(piece, piece, s3_s.at[half, k], s3_r.at[half, k], at(core_=other))

    def s3_arrival(half, k):
        piece = a.at[other + 2 * half, rotate(y, 4 - k, NY)]
        return copy(piece, piece, s3_s.at[half, k], s3_r.at[half, k], at(core_=other))

    for half in (0, 1):
        copy(hg, a.at[core + 2 * half, y], s1_s.at[0], s1_r.at[half], at(core_=other)).wait_recv()
        for k in (1, 3, 2):
            s2_copy(half, k).start()
    for half in (0, 1):
        s3_copy(half, 0).start()
    reduce_zl(0)
    pump(0)
    w_send(2)
    reduce_y(0)
    pump(1)
    w_send(3)
    for half in (0, 1):
        for k in (1, 3, 2):
            s2_arrival(half, k).wait_recv()
            s3_copy(half, k).start()
    total = reduce_end(0)
    inv = 1.0 / jnp.sqrt(spread(total[:1]) / (NX * NZ * feats) + EPS)
    inv_ref[...] = inv
    racc[...] = jnp.zeros_like(racc)
    for half in (0, 1):
        for k in range(4):
            s3_arrival(half, k).wait_recv()
    own_w.wait()

    def rs_copy(c, j):
        return copy(part_send.at[c, j], rs_recv.at[c, j], rs_s.at[c, j], rs_r.at[c, j], at(x_=rotate(x, 1 + j, NX)))

    def ag_copy(c, j):
        return copy(ag.at[c, x], ag.at[c, x], ag_s.at[c, j], ag_r.at[c, j], at(x_=rotate(x, 1 + j, NX)))

    def ag_arrival(c, j):
        piece = ag.at[c, rotate(x, 3 - j, NX)]
        return copy(piece, piece, ag_s.at[c, j], ag_r.at[c, j], at(x_=rotate(x, 1 + j, NX)))

    def project(c):
        for up in (True, False):
            w_forward(c, up).wait_recv()

        def one(j):
            xs = rotate(x, 1 + j, NX)
            acc = jnp.zeros((rows, cols), F32)
            for r in range(4):
                acc = acc + jnp.dot(a[xs, rotate(zh, r, NZ)], wg[r, c], preferred_element_type=F32)
            return acc

        def send(j, carry):
            part_send[c, j] = one(j).astype(BF16)
            rs_copy(c, j).start()
            return carry

        lax.fori_loop(0, 3, send, 0)
        own_part[c] = one(3)

    lane = lax.broadcasted_iota(jnp.int32, (1, 128), 1)
    first = lane < HEAD_DIM

    def two_heads(v):
        return jnp.concatenate([jnp.where(first, v, 0.0), jnp.where(first, 0.0, v)], axis=0).astype(BF16)

    def per_head(v, f):
        return jnp.concatenate([f(v[:, :src]), f(v[:, src:])], axis=1)

    def dot_t(m, n):
        return lax.dot_general(m, n, (((1,), (1,)), ((), ())), preferred_element_type=F32)

    def t_dot(m, n):
        return lax.dot_general(m, n, (((0,), (0,)), ((), ())), preferred_element_type=F32)

    def attend(c):
        for j in range(3):
            rs_copy(c, j).wait_recv()
        kv = own_part[c]
        for j in range(3):
            kv = kv + rs_recv[c, j].astype(F32)
        kvf[...] = kv * jnp.concatenate([inv_ref[...]] * (cols // 128), axis=1)
        lanes = pl.ds(pl.multiple_of(c * 128, 128), 128)

        def one(b, carry):
            at_rows = pl.ds(pl.multiple_of(b * src, src), src)
            kv_b = kvf[at_rows, :]
            keys = two_heads(kv_b[:, :128].astype(BF16).astype(F32))
            values = two_heads(kv_b[:, 128:].astype(BF16).astype(F32))
            query, cotan = q_ref[b, :, lanes], og_ref[b, :, lanes]
            expo = jnp.exp(dot_t(query, keys) * SCALE + bias_ref[b, :1, :])
            probs = per_head(expo, lambda e: e / jnp.sum(e, axis=-1, keepdims=True))
            probs_b = probs.astype(BF16)
            att_ref[b, :, lanes] = jnp.dot(probs_b, values, preferred_element_type=F32).astype(BF16)
            dprob = dot_t(cotan, values)
            delta = per_head(
                probs * dprob, lambda e: jnp.broadcast_to(jnp.sum(e, axis=-1, keepdims=True), e.shape)
            )
            dscore = (probs * (dprob - delta) * SCALE).astype(BF16)
            gq_ref[b, :, lanes] = jnp.dot(dscore, keys, preferred_element_type=F32).astype(BF16)
            dkey, dvalue = t_dot(dscore, query), t_dot(probs_b, cotan)
            dkv = jnp.concatenate(
                [jnp.where(first, dkey[:src], dkey[src:]), jnp.where(first, dvalue[:src], dvalue[src:])], axis=1
            ).astype(BF16)
            ag[c, x, at_rows, :] = dkv
            product = dkv.astype(F32) * kv_b
            racc[at_rows, :] = racc[at_rows, :] + (product[:, :128] + product[:, 128:])
            return carry

        lax.fori_loop(0, batches, one, 0)
        for j in range(3):
            ag_copy(c, j).start()

    def back(c):
        for j in range(3):
            ag_arrival(c, j).wait_recv()

        def one(i, carry):
            xs, r = i // 4, lax.rem(i, 4)
            term = dot_t(ag[c, xs], wg[r, c])

            @pl.when(c == 0)
            def _():
                dn[xs, r] = term

            @pl.when(c > 0)
            def _():
                dn[xs, r] = dn[xs, r] + term

            return carry

        lax.fori_loop(0, 16, one, 0)

    def turn(i, carry):
        @pl.when(i < CHUNKS)
        def _():
            project(i)

        @pl.when(i + 2 < CHUNKS)
        def _():
            pump(i + 2)

        @pl.when(jnp.logical_and(i >= 1, i <= CHUNKS))
        def _():
            attend(i - 1)

        @pl.when(i >= 2)
        def _():
            back(i - 2)

        return carry

    lax.fori_loop(0, CHUNKS + 1, turn, 0)
    reduce_start(8, total_lanes(racc[...]))
    back(CHUNKS - 1)

    def d1_copy(half, r):
        return copy(core_send.at[half, r], core_recv.at[half, r], d1_s.at[half, r], d1_r.at[half, r], at(core_=other))

    def d1_send(i, carry):
        half, r = i // 4, lax.rem(i, 4)
        core_send[half, r] = dn[other + 2 * half, r].astype(BF16)
        d1_copy(half, r).start()
        return carry

    lax.fori_loop(0, 8, d1_send, 0)
    reduce_zl(8)

    def d2_copy(half, k):
        return copy(
            y_send.at[half, k - 1], y_recv.at[half, k - 1], d2_s.at[half, k - 1], d2_r.at[half, k - 1],
            at(y_=rotate(y, k, NY)),
        )

    def chip_sum(half, r):
        d1_copy(half, r).wait_recv()
        return dn[core + 2 * half, r] + core_recv[half, r].astype(F32)

    def d2_send(i, carry):
        half, k = i // 3, lax.rem(i, 3) + 1
        y_send[half, k - 1] = chip_sum(half, lax.rem(y + k + NZ - zh, NZ)).astype(BF16)
        d2_copy(half, k).start()
        return carry

    lax.fori_loop(0, 6, d2_send, 0)
    for half in (0, 1):
        y_own[half] = chip_sum(half, lax.rem(y + NZ - zh, NZ))
    reduce_y(8)
    total = reduce_end(8)
    inv = inv_ref[...]
    rsum_ref[...] = spread(total[:1]) * inv * inv / (NX * NZ * feats)

    def d3_copy(half):
        to = (y, zh * 4 + core + 2 * half, x)
        return copy(fin_send.at[half], fin.at[zl], d3_s.at[half], d3_r.at[zl], to)

    for half in (0, 1):
        for k in (1, 2, 3):
            d2_copy(half, k).wait_recv()
        v = y_own[half]
        for k in range(3):
            v = v + y_recv[half, k].astype(F32)
        fin_send[half] = v.astype(BF16)
        stays = jnp.logical_and(home, x // 2 == half)

        @pl.when(stays)
        def _():
            pltpu.make_async_copy(fin_send.at[half], fin.at[zl], d3_r.at[zl]).start()

        @pl.when(jnp.logical_not(stays))
        def _():
            d3_copy(half).start()

    for k in (0, 1):
        copy(fin_send.at[0], fin.at[k], d3_s.at[0], d3_r.at[k], at(core_=other)).wait_recv()
    dnormed = fin[0].astype(F32) + fin[1].astype(F32)
    h = states_ref[...].astype(F32)
    wide = lambda v: jnp.concatenate([v] * (feats // 128), axis=1)
    inv = wide(inv_ref[...])
    scaled = dnormed * inv

    def gain_copy(over_x, k):
        piece = gsum.at[x] if over_x else gsum.at[4 + zh]
        place = k if over_x else 4 + k
        to = at(x_=rotate(x, k, NX)) if over_x else at(zh_=rotate(zh, k, NZ))
        return copy(piece, piece, gs_s.at[place], gs_r.at[place], to)

    def gain_arrival(over_x, k):
        piece = gsum.at[rotate(x, 4 - k, NX)] if over_x else gsum.at[4 + rotate(zh, 4 - k, NZ)]
        place = k if over_x else 4 + k
        to = at(x_=rotate(x, k, NX)) if over_x else at(zh_=rotate(zh, k, NZ))
        return copy(piece, piece, gs_s.at[place], gs_r.at[place], to)

    gsum[x] = jnp.broadcast_to(jnp.sum(scaled * h, axis=0, keepdims=True), (8, feats))
    for k in (1, 2, 3):
        gain_copy(True, k).start()
    gs_ref[...] = gain_ref[...] * scaled - h * wide(rsum_ref[...])
    for k in (1, 2, 3):
        gain_arrival(True, k).wait_recv()
    gsum[4 + zh] = (gsum[0] + gsum[1]) + (gsum[2] + gsum[3])
    for k in (1, 2, 3):
        gain_copy(False, k).start()

    def sent_w(c, carry):
        for up in (True, False):
            w_direct(c, up).wait_send()
            w_forward(c, up).wait_send()
        for j in range(3):
            rs_copy(c, j).wait_send()
            ag_copy(c, j).wait_send()
        return carry

    lax.fori_loop(0, CHUNKS, sent_w, 0)
    s1_far.wait_send()

    @pl.when(jnp.logical_not(home))
    def _():
        s1_near.wait_send()

    for half in (0, 1):
        for k in (1, 2, 3):
            s2_copy(half, k).wait_send()
            d2_copy(half, k).wait_send()
        for k in range(4):
            s3_copy(half, k).wait_send()
            d1_copy(half, k).wait_send()

        @pl.when(jnp.logical_not(jnp.logical_and(home, x // 2 == half)))
        def _():
            d3_copy(half).wait_send()

    for k in (1, 2, 3):
        gain_copy(True, k).wait_send()
    for k in (1, 2, 3):
        gain_arrival(False, k).wait_recv()
    gg_ref[...] = (gsum[4] + gsum[5]) + (gsum[6] + gsum[7])
    for k in (1, 2, 3):
        gain_copy(False, k).wait_send()


def per_device(states, gain, kv_weight, queries, out_grad, src_len):
    batches, src, feats = states.shape
    tgt, heads_cols = queries.shape[2:]
    rows = batches * src
    cols = 2 * heads_cols // CHUNKS
    w = kv_weight[0].reshape(feats, 2, CHUNKS, cols // 2).transpose(2, 0, 1, 3).reshape(CHUNKS, feats, cols)
    valid = jnp.arange(src, dtype=jnp.int32)[None, :] < src_len[:, None]
    bias = jnp.where(valid, 0.0, MASKED).astype(F32)
    bias = jnp.broadcast_to(jnp.concatenate([bias, bias], axis=1)[:, None, :], (batches, 8, 2 * src))
    vmem = pl.BlockSpec(memory_space=pltpu.VMEM)
    dma = pltpu.SemaphoreType.DMA
    out = pl.pallas_call(
        kernel,
        out_shape=(
            jax.ShapeDtypeStruct((batches, tgt, heads_cols), BF16),
            jax.ShapeDtypeStruct((batches, tgt, heads_cols), BF16),
            jax.ShapeDtypeStruct((rows, feats), F32),
            jax.ShapeDtypeStruct((8, feats), F32),
        ),
        in_specs=[vmem] * 6,
        out_specs=[vmem] * 4,
        scratch_shapes=[
            pltpu.VMEM((rows, feats), BF16),
            pltpu.VMEM((4, CHUNKS, feats, cols), BF16),
            pltpu.VMEM((4, 4, rows, feats), BF16),
            pltpu.VMEM((CHUNKS, rows, cols), F32),
            pltpu.VMEM((CHUNKS, 3, rows, cols), BF16),
            pltpu.VMEM((CHUNKS, 3, rows, cols), BF16),
            pltpu.VMEM((CHUNKS, 4, rows, cols), BF16),
            pltpu.VMEM((4, 4, rows, feats), F32),
            pltpu.VMEM((2, 4, rows, feats), BF16),
            pltpu.VMEM((2, 4, rows, feats), BF16),
            pltpu.VMEM((2, 3, rows, feats), BF16),
            pltpu.VMEM((2, 3, rows, feats), BF16),
            pltpu.VMEM((2, rows, feats), F32),
            pltpu.VMEM((2, rows, feats), BF16),
            pltpu.VMEM((2, rows, feats), BF16),
            pltpu.VMEM((rows, cols), F32),
            pltpu.VMEM((rows, 128), F32),
            pltpu.VMEM((16, 8, rows), F32),
            pltpu.VMEM((8, 8, feats), F32),
            pltpu.VMEM((rows, 128), F32),
            pltpu.VMEM((rows, 128), F32),
            dma((1,)),
            dma((2, CHUNKS)), dma((2, CHUNKS)), dma((2, CHUNKS)), dma((2, CHUNKS)),
            dma((2,)), dma((2,)),
            dma((2, 3)), dma((2, 3)),
            dma((2, 4)), dma((2, 4)),
            dma((CHUNKS, 3)), dma((CHUNKS, 3)),
            dma((CHUNKS, 3)), dma((CHUNKS, 3)),
            dma((2, 4)), dma((2, 4)),
            dma((2, 3)), dma((2, 3)),
            dma((2,)), dma((2,)),
            dma((16,)), dma((16,)),
            dma((8,)), dma((8,)),
        ],
        compiler_params=pltpu.CompilerParams(
            collective_id=1, has_side_effects=True, vmem_limit_bytes=52 * 2**20
        ),
        name="cross_attention",
    )(
        w, states.reshape(rows, feats), gain.astype(F32).reshape(1, feats), queries[0], out_grad[0], bias
    )
    attended, grad_q, grad_states, grad_gain = out
    return attended[None], grad_q[None], grad_states.reshape(batches, src, feats), grad_gain[0]


def solution(mesh):
    return jax.shard_map(
        per_device,
        mesh=mesh,
        in_specs=(
            P("dp", None, ("section", "tensor")),
            P(("section", "tensor")),
            P("section", "dp", None, "tensor"),
            P("section", "dp", None, "tensor"),
            P("section", "dp", None, "tensor"),
            P("dp"),
        ),
        out_specs=(
            P("section", "dp", None, "tensor"),
            P("section", "dp", None, "tensor"),
            P("dp", None, ("section", "tensor")),
            P(("section", "tensor")),
        ),
        check_vma=False,
    )
```

time: 477 us -> 183 us (0.38)
  waiting for transfers between devices: 313 us -> 0 us
  Pallas kernels: 0 us -> 173 us
  blocking collectives: 88.3 us -> 0 us
  matrix products: 42.4 us -> 0 us
  between operations: 13.9 us -> 0.68 us
  other arithmetic: 6.44 us -> 0.08 us
    all_gather x2 -> x0, waiting for transfers between devices: 222 us -> none  [the longest x1 200 us: per_device(): weights = lax.all_gather(kv_weight, 'dp', axis=1, tiled=True)[0]]
    pallas_call x0 -> x1, Pallas kernels: none -> 173 us  [per_device(): pl.pallas_call(kernel, out_shape=(jax.ShapeDtypeStruct((batches, tgt, hea...]
    reduce_scatter x1 -> x0, waiting for transfers between devices: 90.2 us -> none  [per_device(): lax.psum_scatter(term, ('section', 'tensor'), scatter_dimension=2, tiled=...]
    psum x2 -> x0, blocking collectives: 66.6 us -> none  [the longest x1 37.7 us: per_device(): grad_gain = lax.psum(gain_term, 'dp')]
    dot_general x8 -> x0, matrix products: 42.4 us -> none  [the longest x1 18.8 us: per_device(): jnp.einsum('bsch,dch->bsd', dkv, weights, preferred_element_type=jnp.floa...]
    all_gather x1 -> x0, blocking collectives: 21.7 us -> none  [per_device(): lax.all_gather(gain, ('section', 'tensor'), axis=0, tiled=True)]
  transfers between devices with their start and end apart: 3 -> 0, of which waited for: 3 -> 0; matrix products, arithmetic and copies ran while one was open for 3% -> 0% of each run, Pallas kernels for 0% -> 0%
where the time goes in v1:
time: 183 us; the launch traced here: 182 us
  Pallas kernels  173 us (95%)
  local copies, waits for them, and re-layouts  8.31 us (5%)
    pallas_call x1, Pallas kernels, per_device(): pl.pallas_call(kernel, out_shape=(jax.ShapeDtypeStruct((batches, tgt, hea...  173 us
    unnamed x9, local copies, waits for them, and re-layouts  3.71 us

profile of v1, /device:TPU:1, one launch (start us, length us, event | category | flops | bytes accessed | tf_op | source)
XLA Modules:
  0.0 181.8 jit_solution(14557765929869476801)
XLA Ops:
  0.6 0.0 copy-start.2
  0.6 0.6 copy-done.2
  1.3 0.1 compare_select_fusion
  1.4 0.0 copy-start.1
  1.4 0.7 copy-done.1
  2.0 1.7 reshape_squeeze.3
  3.8 0.8 copy.12
  4.6 0.0 copy-start
  4.6 1.5 reshape.24.w_ref
  6.1 0.0 copy-done
  6.1 172.7 %cross_attention.1 = (bf16[2,256,512]{2,1,0:T(8,128)(2,1)S(1)}, bf16[2,256,512]{2,1,0:T(8,128)(2,1)S(1)}, f32[256,512]{1,0:T(8,128)S(1)}, f32[8,512]{1,0:T(8,128)S(1)}) custom-call(bf16[4,512,256]{2,1,0:T(8,128)(2,1)} %reshape.24.w_ref, bf16[256,512]{1,0:T(8,128)(2,1)S(1)} %bitcast.14, f32[1,512]{1,0:T(1,128)S(1)} %bitcast.15, ...), custom_call_target="tpu_custom_call" | custom-call | tf_op jit(solution)/shard_map/cross_attention/pallas_call | solution.py:466
  178.8 0.6 slice.3
  179.4 0.8 copy.16
  180.2 0.8 copy.17
  181.0 0.8 copy.18
  (3 shorter events, 0.0 us)
Async XLA Ops:
  0.6 0.7 copy-start.2
  1.4 0.7 copy-start.1
  4.6 1.5 copy-start

commit v2 on v1

v2 whole, which is shorter than its diff:
```python
import jax
import jax.numpy as jnp
from jax import lax
from jax.experimental import pallas as pl
from jax.experimental.pallas import tpu as pltpu
from jax.sharding import PartitionSpec as P

MESH = pl.DeviceIdType.MESH
HEAD_DIM = 64
SCALE = HEAD_DIM ** (-0.5)
EPS = 1e-06
NX, NY, NZ = 4, 4, 4
CHUNKS = 4
F32, BF16 = jnp.float32, jnp.bfloat16


def rotate(a, by, n):
    return lax.rem(a + by, n)


def kernel(
    w_ref, ext_ref, q_in, og_in, len_ref,
    att_ref, gq_ref, gs_ref, gg_ref,
    ext, q_ref, og_ref, wg, raw, a, own_part, part_send, rs_recv, ag, dn, core_send, core_recv, z_send, z_recv, y_send, y_recv,
    y_own, fin_send, fin, racc, small, xtot, gz, gx, inv_ref, piece_inv, rsum_ref,
    local_sem, wd_s, wd_r, wf_s, wf_r, s1_s, s1_r, s2_s, s2_r, s2f_s, s2f_r, s3_s, s3_r, rs_s, rs_r, ag_s, ag_r,
    d1_s, d1_r, dz_s, dz_r, d2_s, d2_r, d3_s, d3_r, sm_s, sm_r, xt_s, xt_r, gz_s, gz_r, gx_s, gx_r,
):
    y, d, t = lax.axis_index("section"), lax.axis_index("dp"), lax.axis_index("tensor")
    zh, x, zl, core = d // 4, lax.rem(d, 4), t // 2, lax.rem(t, 2)
    rows, feats = gs_ref.shape
    batches = q_ref.shape[0]
    src = rows // batches
    cols = wg.shape[3]
    heads_cols = q_ref.shape[2]
    width = NX * NZ * feats

    def at(y_=None, zh_=None, x_=None, zl_=None, core_=None):
        pick = lambda new, old: old if new is None else new
        return (pick(y_, y), pick(zh_, zh) * 4 + pick(x_, x), pick(zl_, zl) * 2 + pick(core_, core))

    def copy(src_ref, dst_ref, send, recv, to):
        return pltpu.make_async_remote_copy(
            src_ref=src_ref, dst_ref=dst_ref, send_sem=send, recv_sem=recv, device_id=to, device_id_type=MESH
        )

    other = 1 - core
    home = t == x

    load_ext = pltpu.make_async_copy(ext_ref, ext, local_sem.at[0])
    load_q = pltpu.make_async_copy(q_in, q_ref, local_sem.at[1])
    load_og = pltpu.make_async_copy(og_in, og_ref, local_sem.at[2])
    load_ext.start()
    load_q.start()
    load_og.start()
    barrier = pltpu.get_barrier_semaphore()

    def greet(to):
        pl.semaphore_signal(barrier, inc=1, device_id=to, device_id_type=MESH)

    for k in (1, 2, 3):
        greet(at(zh_=rotate(zh, k, NZ)))
        greet(at(y_=rotate(y, k, NY)))
        greet(at(x_=rotate(x, k, NX)))
    greet(at(core_=other))
    greet(at(zl_=1 - zl))
    for zl_ in (0, 1):
        for core_ in (0, 1):
            itself = jnp.logical_and(home, jnp.logical_and(zl == zl_, core == core_))

            @pl.when(jnp.logical_not(itself))
            def _():
                greet(at(x_=t, zl_=zl_, core_=core_))

    for x_ in range(NX):

        @pl.when(jnp.logical_not(jnp.logical_and(home, x == x_)))
        def _():
            greet((y, zh * 4 + x_, x))

    @pl.when(jnp.logical_not(home))
    def _():
        pl.semaphore_wait(barrier, 19)

    @pl.when(home)
    def _():
        pl.semaphore_wait(barrier, 17)

    x_core = lax.rem(x, 2)

    def w_lanes(c):
        k = pl.ds(pl.multiple_of(c * 128, 128), 128)
        v = pl.ds(pl.multiple_of(heads_cols + c * 128, 128), 128)
        return ((k, pl.ds(0, 128)), (v, pl.ds(128, 128)))

    def w_direct(c, up):
        to = at(zh_=rotate(zh, 1 if up else 3, NZ))
        piece = wg.at[3 if up else 1, c]
        return copy(piece, piece, wd_s.at[int(up), c], wd_r.at[int(up), c], to)

    def w_forward(c, up):
        half = feats // 2
        part = pl.ds(0 if up else half, half)
        to = at(zh_=rotate(zh, 1 if up else 3, NZ))
        return copy(
            wg.at[3 if up else 1, c, part], wg.at[2, c, part], wf_s.at[int(up), c], wf_r.at[int(up), c], to
        )

    def pump(c):
        for up in (True, False):
            w_direct(c, up).wait_recv()
            w_forward(c, up).start()

    def w_send(c):
        for up in (True, False):
            to = at(zh_=rotate(zh, 1 if up else 3, NZ))
            for here, there in w_lanes(c):
                copy(
                    w_ref.at[:, here], wg.at[3 if up else 1, c, :, there],
                    wd_s.at[int(up), c], wd_r.at[int(up), c], to,
                ).start()

    load_ext.wait()

    def s1_copy(z, to):
        return copy(ext, raw.at[x // 2, y], s1_s.at[z], s1_r.at[x // 2], to)

    s1_far = s1_copy(1, at(x_=t, zl_=1 - zl, core_=x_core))
    s1_near = s1_copy(0, at(x_=t, core_=x_core))
    s1_local = pltpu.make_async_copy(ext, raw.at[x // 2, y], s1_r.at[x // 2])
    s1_far.start()

    @pl.when(jnp.logical_not(home))
    def _():
        s1_near.start()

    @pl.when(home)
    def _():
        s1_local.start()

    for c in range(CHUNKS):
        for here, there in w_lanes(c):
            pltpu.make_async_copy(w_ref.at[:, here], wg.at[0, c, :, there], local_sem.at[3]).start()

    h = ext[:rows, :].astype(F32)
    squares = h * h

    def total_lanes(v):
        acc = v[:, :128]
        for k in range(128, v.shape[1], 128):
            acc = acc + v[:, k : k + 128]
        return jnp.broadcast_to(jnp.sum(acc.T, axis=0, keepdims=True), (8, rows))

    def spread(row):
        return jnp.broadcast_to(row, (128, rows)).T

    def reduce_start(base, v):
        small[base] = v
        c = copy(small.at[base], small.at[base + 1], sm_s.at[base], sm_r.at[base + 1], at(core_=other))
        c.start()

    def reduce_zl(base):
        copy(small.at[base], small.at[base + 1], sm_s.at[base], sm_r.at[base + 1], at(core_=other)).wait()
        small[base + 2] = small[base] + small[base + 1]
        copy(small.at[base + 2], small.at[base + 3], sm_s.at[base + 2], sm_r.at[base + 3], at(zl_=1 - zl)).start()

    def reduce_y_copies(base):
        return [
            copy(
                small.at[base + 4], small.at[base + 4 + k], sm_s.at[base + 4 + k], sm_r.at[base + 4 + k],
                at(y_=rotate(y, k, NY)),
            )
            for k in (1, 2, 3)
        ]

    def reduce_y(base):
        copy(small.at[base + 2], small.at[base + 3], sm_s.at[base + 2], sm_r.at[base + 3], at(zl_=1 - zl)).wait()
        small[base + 4] = small[base + 2] + small[base + 3]
        for c in reduce_y_copies(base):
            c.start()

    def reduce_end(base):
        for c in reduce_y_copies(base):
            c.wait()
        return (small[base + 4] + small[base + 5]) + (small[base + 6] + small[base + 7])

    reduce_start(0, total_lanes(squares))

    cut = 9 * 16
    parts = (pl.ds(0, cut), pl.ds(cut, raw.shape[2] - cut))

    def s2_direct(half, up):
        to = at(y_=rotate(y, 1 if up else 3, NY))
        piece = raw.at[half, y]
        return copy(piece, piece, s2_s.at[half, int(up)], s2_r.at[half, int(up)], to)

    def s2_arrival(half, up):
        to = at(y_=rotate(y, 1 if up else 3, NY))
        piece = raw.at[half, rotate(y, 3 if up else 1, NY)]
        return copy(piece, piece, s2_s.at[half, int(up)], s2_r.at[half, int(up)], to)

    def s2_forward(half, up):
        to = at(y_=rotate(y, 1 if up else 3, NY))
        piece = raw.at[half, rotate(y, 3 if up else 1, NY), parts[0 if up else 1]]
        return copy(piece, piece, s2f_s.at[half, int(up)], s2f_r.at[half, int(up)], to)

    def s2_last(half, up):
        to = at(y_=rotate(y, 1 if up else 3, NY))
        piece = raw.at[half, rotate(y, 2, NY), parts[0 if up else 1]]
        return copy(piece, piece, s2f_s.at[half, int(up)], s2f_r.at[half, int(up)], to)

    def s3_copy(half, k):
        piece = a.at[core + 2 * half, rotate(y, 4 - k, NY)]
        return copy(piece, piece, s3_s.at[half, k], s3_r.at[half, k], at(core_=other))

    def s3_arrival(half, k):
        piece = a.at[other + 2 * half, rotate(y, 4 - k, NY)]
        return copy(piece, piece, s3_s.at[half, k], s3_r.at[half, k], at(core_=other))

    def normalise(half, k):
        s = rotate(y, 4 - k, NY)
        g = raw[half, s, rows : rows + 16, :].astype(F32)[:1]
        v = raw[half, s, :rows, :].astype(F32) * wide(piece_inv[half]) * g
        a[core + 2 * half, s] = v.astype(BF16)
        s3_copy(half, k).start()

    def wide(v):
        return jnp.concatenate([v] * (feats // 128), axis=1)

    def inverse(row):
        return 1.0 / jnp.sqrt(spread(row) / width + EPS)

    def xt_copy(k):
        return copy(xtot.at[x], xtot.at[x], xt_s.at[k - 1], xt_r.at[k - 1], at(x_=rotate(x, k, NX)))

    def xt_arrival(k):
        piece = xtot.at[rotate(x, 4 - k, NX)]
        return copy(piece, piece, xt_s.at[k - 1], xt_r.at[k - 1], at(x_=rotate(x, k, NX)))

    reduce_zl(0)
    s1_far.wait_send()
    w_send(0)
    reduce_y(0)
    for half in (0, 1):
        copy(ext, raw.at[half, y], s1_s.at[0], s1_r.at[half], at(core_=other)).wait_recv()
        for up in (True, False):
            s2_direct(half, up).start()
    w_send(1)
    xtot[x] = reduce_end(0)
    for k in (1, 2, 3):
        xt_copy(k).start()
    for half in (0, 1):
        for up in (True, False):
            s2_arrival(half, up).wait_recv()
            s2_forward(half, up).start()
    pump(0)
    w_send(2)
    for k in (1, 2, 3):
        xt_arrival(k).wait_recv()
    inv_ref[...] = inverse(xtot[x][:1])
    for half in (0, 1):
        piece_inv[half] = inverse(xtot[core + 2 * half][:1])
    racc[...] = jnp.zeros_like(racc)
    for half in (0, 1):
        for k in (0, 1, 3):
            normalise(half, k)
    pump(1)
    w_send(3)
    for half in (0, 1):
        for up in (True, False):
            s2_last(half, up).wait_recv()
        normalise(half, 2)
    load_q.wait()
    load_og.wait()
    pltpu.make_async_copy(wg.at[0], wg.at[0], local_sem.at[3]).wait()
    for half in (0, 1):
        for k in (0, 1, 3, 2):
            s3_arrival(half, k).wait_recv()

    def sequence(b):
        return pl.ds(pl.multiple_of(b * src, src), src)

    def rs_copy(c, j, b):
        part = sequence(b)
        return copy(
            part_send.at[c, j, part], rs_recv.at[c, j, part], rs_s.at[c, j, b], rs_r.at[c, j, b],
            at(x_=rotate(x, 1 + j, NX)),
        )

    def ag_copy(c, j, b):
        piece = ag.at[c, x, sequence(b)]
        return copy(piece, piece, ag_s.at[c, j, b], ag_r.at[c, j, b], at(x_=rotate(x, 1 + j, NX)))

    def ag_arrival(c, j, b):
        piece = ag.at[c, rotate(x, 3 - j, NX), sequence(b)]
        return copy(piece, piece, ag_s.at[c, j, b], ag_r.at[c, j, b], at(x_=rotate(x, 1 + j, NX)))

    def project(c):
        for up in (True, False):
            w_forward(c, up).wait_recv()

        def one(j):
            xs = rotate(x, 1 + j, NX)
            acc = jnp.zeros((rows, cols), F32)
            for r in range(4):
                acc = acc + jnp.dot(a[xs, rotate(zh, r, NZ)], wg[r, c], preferred_element_type=F32)
            return acc

        def send(j, carry):
            part_send[c, j] = one(j).astype(BF16)
            for b in range(batches):
                rs_copy(c, j, b).start()
            return carry

        lax.fori_loop(0, 3, send, 0)
        own_part[c] = one(3)

    lane = lax.broadcasted_iota(jnp.int32, (1, 128), 1)
    first = lane < HEAD_DIM
    place = lax.rem(lax.broadcasted_iota(jnp.int32, (1, 2 * src), 1), src)

    def two_heads(v):
        return jnp.concatenate([jnp.where(first, v, 0.0), jnp.where(first, 0.0, v)], axis=0).astype(BF16)

    def per_head(v, f):
        return jnp.concatenate([f(v[:, :src]), f(v[:, src:])], axis=1)

    def dot_t(m, n):
        return lax.dot_general(m, n, (((1,), (1,)), ((), ())), preferred_element_type=F32)

    def t_dot(m, n):
        return lax.dot_general(m, n, (((0,), (0,)), ((), ())), preferred_element_type=F32)

    def attend(c):
        lanes = pl.ds(pl.multiple_of(c * 128, 128), 128)

        def one(b, carry):
            at_rows = sequence(b)
            kv_b = own_part[c, at_rows, :]
            for j in range(3):
                rs_copy(c, j, b).wait_recv()
                kv_b = kv_b + rs_recv[c, j, at_rows, :].astype(F32)
            keys = two_heads(kv_b[:, :128].astype(BF16).astype(F32))
            values = two_heads(kv_b[:, 128:].astype(BF16).astype(F32))
            query, cotan = q_ref[b, :, lanes], og_ref[b, :, lanes]
            expo = jnp.where(place < len_ref[b], jnp.exp(dot_t(query, keys) * SCALE), 0.0)
            probs = per_head(expo, lambda e: e / jnp.sum(e, axis=-1, keepdims=True))
            probs_b = probs.astype(BF16)
            att_ref[b, :, lanes] = jnp.dot(probs_b, values, preferred_element_type=F32).astype(BF16)
            dprob = dot_t(cotan, values)
            delta = per_head(
                probs * dprob, lambda e: jnp.broadcast_to(jnp.sum(e, axis=-1, keepdims=True), e.shape)
            )
            dscore = (probs * (dprob - delta) * SCALE).astype(BF16)
            gq_ref[b, :, lanes] = jnp.dot(dscore, keys, preferred_element_type=F32).astype(BF16)
            dkey, dvalue = t_dot(dscore, query), t_dot(probs_b, cotan)
            dkv = jnp.concatenate(
                [jnp.where(first, dkey[:src], dkey[src:]), jnp.where(first, dvalue[:src], dvalue[src:])], axis=1
            ).astype(BF16)
            ag[c, x, at_rows, :] = dkv
            for j in range(3):
                ag_copy(c, j, b).start()
            product = dkv.astype(F32) * kv_b
            racc[at_rows, :] = racc[at_rows, :] + (product[:, :128] + product[:, 128:])
            return carry

        lax.fori_loop(0, batches, one, 0)

    def back(chunks):
        for c in chunks:
            for j in range(3):
                for b in range(batches):
                    ag_arrival(c, j, b).wait_recv()

        def one(i, carry):
            xs, r = i // 4, lax.rem(i, 4)
            term = dot_t(ag[chunks[0], xs], wg[r, chunks[0]])
            for c in chunks[1:]:
                term = term + dot_t(ag[c, xs], wg[r, c])
            dn[xs, r] = term if chunks[0] == 0 else dn[xs, r] + term
            return carry

        lax.fori_loop(0, 16, one, 0)

    project(0)
    pump(2)
    attend(0)
    project(1)
    attend(1)
    pump(3)
    project(2)
    back((0, 1))
    attend(2)
    project(3)
    attend(3)
    reduce_start(8, total_lanes(racc[...]))
    back((2,))
    reduce_zl(8)
    last = CHUNKS - 1

    def d1_copy(b, half, k):
        part = sequence(b)
        return copy(
            core_send.at[half, k, part], core_recv.at[half, k, part],
            d1_s.at[b, half, k], d1_r.at[b, half, k], at(core_=other),
        )

    def d2_copy(b, half, k):
        part = sequence(b)
        return copy(
            y_send.at[half, k - 1, part], y_recv.at[half, k - 1, part],
            d2_s.at[b, half, k - 1], d2_r.at[b, half, k - 1], at(y_=rotate(y, k, NY)),
        )

    def whole(b, xs, k):
        part = sequence(b)
        r = lax.rem(y + k + NZ - zh, NZ)
        return dn[xs, r, part, :] + dot_t(ag[last, xs, part, :], wg[r, last])

    def dz_copy(b):
        part = sequence(b)
        return copy(z_send.at[part], z_recv.at[part], dz_s.at[b], dz_r.at[b], at(zl_=1 - zl))

    def chip_sum(b, half, k):
        v = whole(b, core + 2 * half, k)
        d1_copy(b, half, k).wait_recv()
        return v + core_recv[half, k, sequence(b), :].astype(F32)

    for b in range(batches):
        part = sequence(b)
        for j in range(3):
            ag_arrival(last, j, b).wait_recv()
        for k in (2, 1, 3, 0):
            for half in (0, 1):
                core_send[half, k, part, :] = whole(b, other + 2 * half, k).astype(BF16)
                d1_copy(b, half, k).start()
        if b == 0:
            reduce_y(8)
        z_send[part, :] = chip_sum(b, 1 - zl, 2).astype(BF16)
        dz_copy(b).start()
        for half in (0, 1):
            for k in (1, 3):
                y_send[half, k - 1, part, :] = chip_sum(b, half, k).astype(BF16)
                d2_copy(b, half, k).start()
        v = chip_sum(b, zl, 2)
        dz_copy(b).wait_recv()
        y_send[0, 1, part, :] = (v + z_recv[part, :].astype(F32)).astype(BF16)
        d2_copy(b, 0, 2).start()
        for half in (0, 1):
            y_own[half, part, :] = chip_sum(b, half, 0)
    inv = inv_ref[...]
    rsum_ref[...] = spread(reduce_end(8)[:1]) * inv * inv / width

    def d3_copy(b, half):
        part = pl.ds(b * src, src)
        to = (y, zh * 4 + core + 2 * half, x)
        return copy(fin_send.at[half, part], fin.at[zl, part], d3_s.at[b, half], d3_r.at[b, zl], to)

    def stays(half):
        return jnp.logical_and(home, x // 2 == half)

    gain_sum = jnp.zeros((1, feats), F32)
    for b in range(batches):
        part = pl.ds(b * src, src)
        for half in (0, 1):
            v = y_own[half, part, :]
            for k in (1, 3):
                d2_copy(b, half, k).wait_recv()
                v = v + y_recv[half, k - 1, part, :].astype(F32)
            if half == 0:
                d2_copy(b, 0, 2).wait_recv()
            v = v + jnp.where(zl == half, y_recv[0, 1, part, :].astype(F32), 0.0)
            fin_send[half, part, :] = v.astype(BF16)

            @pl.when(stays(half))
            def _():
                pltpu.make_async_copy(fin_send.at[half, part], fin.at[zl, part], d3_r.at[b, zl]).start()

            @pl.when(jnp.logical_not(stays(half)))
            def _():
                d3_copy(b, half).start()

            hidden = raw[half, y, part, :].astype(F32) * wide(piece_inv[half, part, :])
            gain_sum = gain_sum + jnp.sum(v * hidden, axis=0, keepdims=True)

    def gz_copy(k):
        return copy(gz.at[zh], gz.at[zh], gz_s.at[k - 1], gz_r.at[k - 1], at(zh_=rotate(zh, k, NZ)))

    def gz_arrival(k):
        piece = gz.at[rotate(zh, 4 - k, NZ)]
        return copy(piece, piece, gz_s.at[k - 1], gz_r.at[k - 1], at(zh_=rotate(zh, k, NZ)))

    def gx_copy(x_):
        place = 2 * zl + core
        return copy(gz.at[4], gx.at[place], gx_s.at[x_], gx_r.at[place], (y, zh * 4 + x_, x))

    gz[zh] = jnp.broadcast_to(gain_sum, (8, feats))
    for k in (1, 2, 3):
        gz_copy(k).start()

    def owned(b):
        part = pl.ds(b * src, src)
        for k in (0, 1):
            copy(fin_send.at[0, part], fin.at[k, part], d3_s.at[b, 0], d3_r.at[b, k], at(core_=other)).wait_recv()
        dnormed = fin[0, part, :].astype(F32) + fin[1, part, :].astype(F32)
        own_gain = ext[rows : rows + 16, :].astype(F32)[:1]
        gs_ref[part, :] = own_gain * (wide(inv_ref[part, :]) * dnormed) - ext[part, :].astype(F32) * wide(
            rsum_ref[part, :]
        )

    owned(0)
    for k in (1, 2, 3):
        gz_arrival(k).wait_recv()
    gz[4] = (gz[0] + gz[1]) + (gz[2] + gz[3])
    for x_ in range(NX):
        itself = jnp.logical_and(home, x == x_)

        @pl.when(itself)
        def _():
            place = 2 * zl + core
            pltpu.make_async_copy(gz.at[4], gx.at[place], gx_r.at[place]).start()

        @pl.when(jnp.logical_not(itself))
        def _():
            gx_copy(x_).start()

    owned(1)

    def sent_w(c, carry):
        for up in (True, False):
            w_direct(c, up).wait_send()
            w_forward(c, up).wait_send()
        for j in range(3):
            for b in range(batches):
                rs_copy(c, j, b).wait_send()
                ag_copy(c, j, b).wait_send()
        return carry

    lax.fori_loop(0, CHUNKS, sent_w, 0)

    @pl.when(jnp.logical_not(home))
    def _():
        s1_near.wait_send()

    for half in (0, 1):
        for up in (True, False):
            s2_direct(half, up).wait_send()
            s2_forward(half, up).wait_send()
        for k in range(4):
            s3_copy(half, k).wait_send()
        for b in range(batches):
            for k in range(4):
                d1_copy(b, half, k).wait_send()
            for k in (1, 3) if half else (1, 2, 3):
                d2_copy(b, half, k).wait_send()
            if half == 0:
                dz_copy(b).wait_send()

            @pl.when(jnp.logical_not(stays(half)))
            def _():
                d3_copy(b, half).wait_send()

    for k in (1, 2, 3):
        xt_copy(k).wait_send()
        gz_copy(k).wait_send()
    for x_ in range(NX):

        @pl.when(jnp.logical_not(jnp.logical_and(home, x == x_)))
        def _():
            gx_copy(x_).wait_send()

    for k in range(4):
        copy(gz.at[4], gx.at[k], gx_s.at[0], gx_r.at[k], at(core_=other)).wait_recv()
    gg_ref[...] = ((gx[0] + gx[1]) + (gx[2] + gx[3]))[:1]


def per_device(states, gain, kv_weight, queries, out_grad, src_len):
    batches, src, feats = states.shape
    tgt, heads_cols = queries.shape[2:]
    rows = batches * src
    cols = 2 * heads_cols // CHUNKS
    w = kv_weight.reshape(feats, 2 * heads_cols)
    ext = jnp.concatenate([states.reshape(rows, feats), jnp.broadcast_to(gain[None, :], (16, feats))], axis=0)
    vmem = pl.BlockSpec(memory_space=pltpu.VMEM)
    dma = pltpu.SemaphoreType.DMA
    out = pl.pallas_call(
        kernel,
        out_shape=(
            jax.ShapeDtypeStruct((batches, tgt, heads_cols), BF16),
            jax.ShapeDtypeStruct((batches, tgt, heads_cols), BF16),
            jax.ShapeDtypeStruct((rows, feats), F32),
            jax.ShapeDtypeStruct((1, feats), F32),
        ),
        in_specs=[pl.BlockSpec(memory_space=pl.ANY)] * 4 + [pl.BlockSpec(memory_space=pltpu.SMEM)],
        out_specs=[vmem] * 4,
        scratch_shapes=[
            pltpu.VMEM((rows + 16, feats), BF16),
            pltpu.VMEM((batches, tgt, heads_cols), BF16),
            pltpu.VMEM((batches, tgt, heads_cols), BF16),
            pltpu.VMEM((4, CHUNKS, feats, cols), BF16),
            pltpu.VMEM((2, 4, rows + 16, feats), BF16),
            pltpu.VMEM((4, 4, rows, feats), BF16),
            pltpu.VMEM((CHUNKS, rows, cols), F32),
            pltpu.VMEM((CHUNKS, 3, rows, cols), BF16),
            pltpu.VMEM((CHUNKS, 3, rows, cols), BF16),
            pltpu.VMEM((CHUNKS, 4, rows, cols), BF16),
            pltpu.VMEM((4, 4, rows, feats), F32),
            pltpu.VMEM((2, 4, rows, feats), BF16),
            pltpu.VMEM((2, 4, rows, feats), BF16),
            pltpu.VMEM((rows, feats), BF16),
            pltpu.VMEM((rows, feats), BF16),
            pltpu.VMEM((2, 3, rows, feats), BF16),
            pltpu.VMEM((2, 3, rows, feats), BF16),
            pltpu.VMEM((2, rows, feats), F32),
            pltpu.VMEM((2, rows, feats), BF16),
            pltpu.VMEM((2, rows, feats), BF16),
            pltpu.VMEM((rows, 128), F32),
            pltpu.VMEM((16, 8, rows), F32),
            pltpu.VMEM((4, 8, rows), F32),
            pltpu.VMEM((5, 8, feats), F32),
            pltpu.VMEM((4, 8, feats), F32),
            pltpu.VMEM((rows, 128), F32),
            pltpu.VMEM((2, rows, 128), F32),
            pltpu.VMEM((rows, 128), F32),
            dma((4,)),
            dma((2, CHUNKS)), dma((2, CHUNKS)), dma((2, CHUNKS)), dma((2, CHUNKS)),
            dma((2,)), dma((2,)),
            dma((2, 2)), dma((2, 2)), dma((2, 2)), dma((2, 2)),
            dma((2, 4)), dma((2, 4)),
            dma((CHUNKS, 3, 2)), dma((CHUNKS, 3, 2)),
            dma((CHUNKS, 3, 2)), dma((CHUNKS, 3, 2)),
            dma((2, 2, 4)), dma((2, 2, 4)),
            dma((2,)), dma((2,)),
            dma((2, 2, 3)), dma((2, 2, 3)),
            dma((2, 2)), dma((2, 2)),
            dma((16,)), dma((16,)),
            dma((3,)), dma((3,)),
            dma((3,)), dma((3,)),
            dma((4,)), dma((4,)),
        ],
        compiler_params=pltpu.CompilerParams(
            collective_id=1, has_side_effects=True, vmem_limit_bytes=52 * 2**20
        ),
        name="cross_attention",
    )(
        w, ext, queries[0], out_grad[0], src_len
    )
    attended, grad_q, grad_states, grad_gain = out
    return attended[None], grad_q[None], grad_states.reshape(batches, src, feats), grad_gain[0]


def solution(mesh):
    return jax.shard_map(
        per_device,
        mesh=mesh,
        in_specs=(
            P("dp", None, ("section", "tensor")),
            P(("section", "tensor")),
            P("section", "dp", None, "tensor"),
            P("section", "dp", None, "tensor"),
            P("section", "dp", None, "tensor"),
            P("dp"),
        ),
        out_specs=(
            P("section", "dp", None, "tensor"),
            P("section", "dp", None, "tensor"),
            P("dp", None, ("section", "tensor")),
            P(("section", "tensor")),
        ),
        check_vma=False,
    )
```

time: 183 us -> 165 us (0.902)
  Pallas kernels: 173 us -> 156 us
    pallas_call x1, Pallas kernels: 173 us -> 156 us  [per_device(): pl.pallas_call(kernel, out_shape=(jax.ShapeDtypeStruct((batches, tgt, hea...]
    unnamed x9, local copies, waits for them, and re-layouts: 3.71 us -> 6.73 us
    another operation x2 -> x0, local copies, waits for them, and re-layouts: 2.54 us -> none  [per_device(): kv_weight[0].reshape(feats, 2, CHUNKS, cols // 2).transpose(2, 0, 1, 3)]
where the time goes in v2:
time: 165 us; the launch traced here: 164 us
  Pallas kernels  156 us (95%)
  local copies, waits for them, and re-layouts  6.74 us (4%)
    pallas_call x1, Pallas kernels, per_device(): pl.pallas_call(kernel, out_shape=(jax.ShapeDtypeStruct((batches, tgt, hea...  156 us
    unnamed x9, local copies, waits for them, and re-layouts  6.73 us

profile of v2, /device:TPU:1, one launch (start us, length us, event | category | flops | bytes accessed | tf_op | source)
XLA Modules:
  0.0 163.9 jit_solution(14075678198678037403)
XLA Ops:
  0.6 0.0 copy-start.1
  0.6 0.7 copy-done.1
  1.3 1.0 pad_maximum_fusion.ext_ref
  2.3 2.4 %copy.10 = bf16[64,8,2,512]{3,1,2,0:T(8,128)(2,1)} copy(bf16[64,8,2,512]{3,2,1,0:T(2,128)(2,1)} %bitcast.15) | data formatting | bytes 2097152
  4.7 0.0 copy-start
  4.7 0.7 copy-done
  5.4 155.5 %cross_attention.1 = (bf16[2,256,512]{2,1,0:T(8,128)(2,1)S(1)}, bf16[2,256,512]{2,1,0:T(8,128)(2,1)S(1)}, f32[256,512]{1,0:T(8,128)S(1)}, f32[1,512]{1,0:T(1,128)S(1)}) custom-call(bf16[512,1024]{1,0:T(8,128)(2,1)} %bitcast.14, bf16[272,512]{1,0:T(8,128)(2,1)S(1)} %pad_maximum_fusion.ext_ref, bf16[2,256,512]{2,1,0:T(8,128)(2,1)} %bitcast.16, ...), custom_call_target="tpu_custom_call" | custom-call | tf_op jit(solution)/shard_map/cross_attention/pallas_call | solution.py:586
  160.9 0.8 copy.15
  161.7 0.8 copy.16
  162.5 0.8 copy.17
  163.3 0.6 copy.18
  (1 shorter events, 0.0 us)
Async XLA Ops:
  0.6 0.7 copy-start.1
  4.7 0.7 copy-start

commit v3 on v2

--- a/solution.py
+++ b/solution.py
@@ -21,10 +21,10 @@
 def kernel(
     w_ref, ext_ref, q_in, og_in, len_ref,
     att_ref, gq_ref, gs_ref, gg_ref,
-    ext, q_ref, og_ref, wg, raw, a, own_part, part_send, rs_recv, ag, dn, core_send, core_recv, z_send, z_recv, y_send, y_recv,
-    y_own, fin_send, fin, racc, small, xtot, gz, gx, inv_ref, piece_inv, rsum_ref,
-    local_sem, wd_s, wd_r, wf_s, wf_r, s1_s, s1_r, s2_s, s2_r, s2f_s, s2f_r, s3_s, s3_r, rs_s, rs_r, ag_s, ag_r,
-    d1_s, d1_r, dz_s, dz_r, d2_s, d2_r, d3_s, d3_r, sm_s, sm_r, xt_s, xt_r, gz_s, gz_r, gx_s, gx_r,
+    ext, q_ref, og_ref, wg, through, through_half, turned, raw, a, own_part, part_send, rs_recv, ag, dn, core_send, core_recv, z_send, z_recv, y_send, y_recv,
+    y_own, fin_send, fin, racc, small, xtot, gz, gy, gx, inv_ref, piece_inv, rsum_ref,
+    local_sem, w_s, w_r, s1_s, s1_r, s2_s, s2_r, s2f_s, s2f_r, s3_s, s3_r, rs_s, rs_r, ag_s, ag_r,
+    d1_s, d1_r, dz_s, dz_r, d2_s, d2_r, d3_s, d3_r, sm_s, sm_r, xt_s, xt_r, gz_s, gz_r, gy_s, gy_r, gx_s, gx_r,
 ):
     y, d, t = lax.axis_index("section"), lax.axis_index("dp"), lax.axis_index("tensor")
     zh, x, zl, core = d // 4, lax.rem(d, 4), t // 2, lax.rem(t, 2)
@@ -63,7 +63,10 @@
         greet(at(y_=rotate(y, k, NY)))
         greet(at(x_=rotate(x, k, NX)))
     greet(at(core_=other))
-    greet(at(zl_=1 - zl))
+    above = at(zh_=rotate(zh, zl, NZ), zl_=1 - zl)
+    below = at(zh_=rotate(zh, 3 + zl, NZ), zl_=1 - zl)
+    greet(above)
+    greet(below)
     for zl_ in (0, 1):
         for core_ in (0, 1):
             itself = jnp.logical_and(home, jnp.logical_and(zl == zl_, core == core_))
@@ -80,11 +83,11 @@
 
     @pl.when(jnp.logical_not(home))
     def _():
-        pl.semaphore_wait(barrier, 19)
+        pl.semaphore_wait(barrier, 20)
 
     @pl.when(home)
     def _():
-        pl.semaphore_wait(barrier, 17)
+        pl.semaphore_wait(barrier, 18)
 
     x_core = lax.rem(x, 2)
 
@@ -93,32 +96,33 @@
         v = pl.ds(pl.multiple_of(heads_cols + c * 128, 128), 128)
         return ((k, pl.ds(0, 128)), (v, pl.ds(128, 128)))
 
-    def w_direct(c, up):
-        to = at(zh_=rotate(zh, 1 if up else 3, NZ))
-        piece = wg.at[3 if up else 1, c]
-        return copy(piece, piece, wd_s.at[int(up), c], wd_r.at[int(up), c], to)
-
-    def w_forward(c, up):
+    def w_copy(stage, c, up):
         half = feats // 2
-        part = pl.ds(0 if up else half, half)
-        to = at(zh_=rotate(zh, 1 if up else 3, NZ))
-        return copy(
-            wg.at[3 if up else 1, c, part], wg.at[2, c, part], wf_s.at[int(up), c], wf_r.at[int(up), c], to
-        )
-
-    def pump(c):
-        for up in (True, False):
-            w_direct(c, up).wait_recv()
-            w_forward(c, up).start()
+        part, rest = pl.ds(0 if up else half, half), pl.ds(half if up else 0, half)
+        way, direct = int(up), wg.at[3 if up else 1, c]
+        here, there = (
+            (through.at[way, c], through.at[way, c]),
+            (through.at[way, c, part], direct.at[part]),
+            (direct.at[part], through_half.at[way, c]),
+            (through_half.at[way, c], wg.at[2, c, part]),
+            (through.at[way, c, rest], direct.at[rest]),
+        )[stage]
+        return copy(here, there, w_s.at[stage, way, c], w_r.at[stage, way, c], above if up else below)
 
     def w_send(c):
         for up in (True, False):
-            to = at(zh_=rotate(zh, 1 if up else 3, NZ))
             for here, there in w_lanes(c):
                 copy(
-                    w_ref.at[:, here], wg.at[3 if up else 1, c, :, there],
-                    wd_s.at[int(up), c], wd_r.at[int(up), c], to,
+                    w_ref.at[:, here], through.at[int(up), c, :, there],
+                    w_s.at[0, int(up), c], w_r.at[0, int(up), c], above if up else below,
                 ).start()
+
+    def hop(stage, c):
+        for up in (True, False):
+            w_copy(stage, c, up).wait_recv()
+            w_copy(stage + 1, c, up).start()
+            if stage == 0:
+                w_copy(4, c, up).start()
 
     load_ext.wait()
 
@@ -249,12 +253,7 @@
     xtot[x] = reduce_end(0)
     for k in (1, 2, 3):
         xt_copy(k).start()
-    for half in (0, 1):
-        for up in (True, False):
-            s2_arrival(half, up).wait_recv()
-            s2_forward(half, up).start()
-    pump(0)
-    w_send(2)
+    hop(0, 0)
     for k in (1, 2, 3):
         xt_arrival(k).wait_recv()
     inv_ref[...] = inverse(xtot[x][:1])
@@ -262,20 +261,31 @@
         piece_inv[half] = inverse(xtot[core + 2 * half][:1])
     racc[...] = jnp.zeros_like(racc)
     for half in (0, 1):
-        for k in (0, 1, 3):
+        normalise(half, 0)
+    hop(0, 1)
+    for half in (0, 1):
+        for up in (True, False):
+            s2_arrival(half, up).wait_recv()
+            s2_forward(half, up).start()
+    hop(1, 0)
+    w_send(2)
+    for half in (0, 1):
+        for k in (1, 3):
             normalise(half, k)
-    pump(1)
-    w_send(3)
+    hop(1, 1)
     for half in (0, 1):
         for up in (True, False):
             s2_last(half, up).wait_recv()
         normalise(half, 2)
+    hop(2, 0)
     load_q.wait()
     load_og.wait()
     pltpu.make_async_copy(wg.at[0], wg.at[0], local_sem.at[3]).wait()
     for half in (0, 1):
         for k in (0, 1, 3, 2):
             s3_arrival(half, k).wait_recv()
+    hop(0, 2)
+    hop(2, 1)
 
     def sequence(b):
         return pl.ds(pl.multiple_of(b * src, src), src)
@@ -297,23 +307,24 @@
 
     def project(c):
         for up in (True, False):
-            w_forward(c, up).wait_recv()
-
-        def one(j):
+            w_copy(4, c, up).wait_recv()
+            w_copy(3, c, up).wait_recv()
+
+        def one(j, b):
             xs = rotate(x, 1 + j, NX)
-            acc = jnp.zeros((rows, cols), F32)
+            acc = jnp.zeros((src, cols), F32)
             for r in range(4):
-                acc = acc + jnp.dot(a[xs, rotate(zh, r, NZ)], wg[r, c], preferred_element_type=F32)
+                acc = acc + jnp.dot(a[xs, rotate(zh, r, NZ), sequence(b), :], wg[r, c], preferred_element_type=F32)
             return acc
 
-        def send(j, carry):
-            part_send[c, j] = one(j).astype(BF16)
-            for b in range(batches):
+        def sequences(b, carry):
+            for j in range(3):
+                part_send[c, j, sequence(b), :] = one(j, b).astype(BF16)
                 rs_copy(c, j, b).start()
+            own_part[c, sequence(b), :] = one(3, b)
             return carry
 
-        lax.fori_loop(0, 3, send, 0)
-        own_part[c] = one(3)
+        lax.fori_loop(0, batches, sequences, 0)
 
     lane = lax.broadcasted_iota(jnp.int32, (1, 128), 1)
     first = lane < HEAD_DIM
@@ -372,31 +383,39 @@
                 for b in range(batches):
                     ag_arrival(c, j, b).wait_recv()
 
-        def one(i, carry):
-            xs, r = i // 4, lax.rem(i, 4)
-            term = dot_t(ag[chunks[0], xs], wg[r, chunks[0]])
+        def one(r, carry):
+            term = dot_t(ag[chunks[0]].reshape(4 * rows, cols), wg[r, chunks[0]])
             for c in chunks[1:]:
-                term = term + dot_t(ag[c, xs], wg[r, c])
-            dn[xs, r] = term if chunks[0] == 0 else dn[xs, r] + term
+                term = term + dot_t(ag[c].reshape(4 * rows, cols), wg[r, c])
+            for xs in range(4):
+                mine = term[xs * rows : (xs + 1) * rows]
+                dn[xs, r] = mine if chunks[0] == 0 else dn[xs, r] + mine
             return carry
 
-        lax.fori_loop(0, 16, one, 0)
+        lax.fori_loop(0, 4, one, 0)
 
     project(0)
-    pump(2)
+    hop(1, 2)
+    w_send(3)
+    project(1)
     attend(0)
-    project(1)
+    hop(2, 2)
     attend(1)
-    pump(3)
+    hop(0, 3)
+    back((0,))
     project(2)
-    back((0, 1))
+    hop(1, 3)
+    back((1,))
+    hop(2, 3)
     attend(2)
     project(3)
     attend(3)
     reduce_start(8, total_lanes(racc[...]))
+    last = CHUNKS - 1
+    for r in range(4):
+        turned[r] = wg[r, last].T
     back((2,))
     reduce_zl(8)
-    last = CHUNKS - 1
 
     def d1_copy(b, half, k):
         part = sequence(b)
@@ -415,7 +434,7 @@
     def whole(b, xs, k):
         part = sequence(b)
         r = lax.rem(y + k + NZ - zh, NZ)
-        return dn[xs, r, part, :] + dot_t(ag[last, xs, part, :], wg[r, last])
+        return dn[xs, r, part, :] + jnp.dot(ag[last, xs, part, :], turned[r], preferred_element_type=F32)
 
     def dz_copy(b):
         part = sequence(b)
@@ -426,10 +445,10 @@
         d1_copy(b, half, k).wait_recv()
         return v + core_recv[half, k, sequence(b), :].astype(F32)
 
-    for b in range(batches):
-        part = sequence(b)
+    def cores(b):
         for j in range(3):
             ag_arrival(last, j, b).wait_recv()
+        part = sequence(b)
         for k in (2, 1, 3, 0):
             for half in (0, 1):
                 core_send[half, k, part, :] = whole(b, other + 2 * half, k).astype(BF16)
@@ -438,18 +457,29 @@
             reduce_y(8)
         z_send[part, :] = chip_sum(b, 1 - zl, 2).astype(BF16)
         dz_copy(b).start()
+
+    def one_step(b):
         for half in (0, 1):
             for k in (1, 3):
-                y_send[half, k - 1, part, :] = chip_sum(b, half, k).astype(BF16)
+                y_send[half, k - 1, sequence(b), :] = chip_sum(b, half, k).astype(BF16)
                 d2_copy(b, half, k).start()
+
+    def two_steps(b):
+        part = sequence(b)
         v = chip_sum(b, zl, 2)
         dz_copy(b).wait_recv()
         y_send[0, 1, part, :] = (v + z_recv[part, :].astype(F32)).astype(BF16)
         d2_copy(b, 0, 2).start()
+
+    cores(0)
+    one_step(0)
+    cores(1)
+    two_steps(0)
+    one_step(1)
+    two_steps(1)
+    for b in range(batches):
         for half in (0, 1):
-            y_own[half, part, :] = chip_sum(b, half, 0)
-    inv = inv_ref[...]
-    rsum_ref[...] = spread(reduce_end(8)[:1]) * inv * inv / width
+            y_own[half, sequence(b), :] = chip_sum(b, half, 0)
 
     def d3_copy(b, half):
         part = pl.ds(b * src, src)
@@ -459,16 +489,16 @@
     def stays(half):
         return jnp.logical_and(home, x // 2 == half)
 
-    gain_sum = jnp.zeros((1, feats), F32)
-    for b in range(batches):
+    def deliver(b):
         part = pl.ds(b * src, src)
+        for k in (1, 3):
+            for half in (0, 1):
+                d2_copy(b, half, k).wait_recv()
+        d2_copy(b, 0, 2).wait_recv()
         for half in (0, 1):
             v = y_own[half, part, :]
             for k in (1, 3):
-                d2_copy(b, half, k).wait_recv()
                 v = v + y_recv[half, k - 1, part, :].astype(F32)
-            if half == 0:
-                d2_copy(b, 0, 2).wait_recv()
             v = v + jnp.where(zl == half, y_recv[0, 1, part, :].astype(F32), 0.0)
             fin_send[half, part, :] = v.astype(BF16)
 
@@ -480,8 +510,13 @@
             def _():
                 d3_copy(b, half).start()
 
-            hidden = raw[half, y, part, :].astype(F32) * wide(piece_inv[half, part, :])
-            gain_sum = gain_sum + jnp.sum(v * hidden, axis=0, keepdims=True)
+    def weighed(v, half, k):
+        hidden = raw[half, rotate(y, k, NY), :rows, :].astype(F32) * wide(piece_inv[half])
+        return jnp.sum(v.astype(F32) * hidden, axis=0, keepdims=True)
+
+    def folded(v):
+        lanes = [v[:, i : i + 128] for i in range(0, feats, 128)]
+        return jnp.concatenate(lanes + lanes, axis=0)
 
     def gz_copy(k):
         return copy(gz.at[zh], gz.at[zh], gz_s.at[k - 1], gz_r.at[k - 1], at(zh_=rotate(zh, k, NZ)))
@@ -490,13 +525,34 @@
         piece = gz.at[rotate(zh, 4 - k, NZ)]
         return copy(piece, piece, gz_s.at[k - 1], gz_r.at[k - 1], at(zh_=rotate(zh, k, NZ)))
 
+    def gy_copy(k):
+        return copy(gz.at[4, k], gy.at[y], gy_s.at[k - 1], gy_r.at[k - 1], at(y_=rotate(y, k, NY)))
+
+    def gy_arrival(k):
+        piece = gy.at[rotate(y, 4 - k, NY)]
+        return copy(piece, piece, gy_s.at[k - 1], gy_r.at[k - 1], at(y_=rotate(y, k, NY)))
+
     def gx_copy(x_):
         place = 2 * zl + core
-        return copy(gz.at[4], gx.at[place], gx_s.at[x_], gx_r.at[place], (y, zh * 4 + x_, x))
-
-    gz[zh] = jnp.broadcast_to(gain_sum, (8, feats))
+        return copy(gy.at[4], gx.at[place], gx_s.at[x_], gx_r.at[place], (y, zh * 4 + x_, x))
+
+    gz[zh, 0] = folded(weighed(y_own[0], 0, 0) + weighed(y_own[1], 1, 0))
+    for k in (1, 3):
+        gz[zh, k] = folded(weighed(y_send[0, k - 1], 0, k) + weighed(y_send[1, k - 1], 1, k))
+    gz[zh, 2] = folded(weighed(y_send[0, 1], zl, 2))
     for k in (1, 2, 3):
         gz_copy(k).start()
+    deliver(0)
+    inv = inv_ref[...]
+    rsum_ref[...] = spread(reduce_end(8)[:1]) * inv * inv / width
+    for k in (1, 2, 3):
+        gz_arrival(k).wait_recv()
+    gz[4] = (gz[0] + gz[1]) + (gz[2] + gz[3])
+    gy[y] = gz[4, 0]
+    for k in (1, 2, 3):
+        gy_copy(k).start()
+
+    deliver(1)
 
     def owned(b):
         part = pl.ds(b * src, src)
@@ -508,28 +564,28 @@
             rsum_ref[part, :]
         )
 
-    owned(0)
     for k in (1, 2, 3):
-        gz_arrival(k).wait_recv()
-    gz[4] = (gz[0] + gz[1]) + (gz[2] + gz[3])
+        gy_arrival(k).wait_recv()
+    gy[4] = (gy[0] + gy[1]) + (gy[2] + gy[3])
     for x_ in range(NX):
         itself = jnp.logical_and(home, x == x_)
 
         @pl.when(itself)
         def _():
             place = 2 * zl + core
-            pltpu.make_async_copy(gz.at[4], gx.at[place], gx_r.at[place]).start()
+            pltpu.make_async_copy(gy.at[4], gx.at[place], gx_r.at[place]).start()
 
         @pl.when(jnp.logical_not(itself))
         def _():
             gx_copy(x_).start()
 
+    owned(0)
     owned(1)
 
     def sent_w(c, carry):
         for up in (True, False):
-            w_direct(c, up).wait_send()
-            w_forward(c, up).wait_send()
+            for stage in range(5):
+                w_copy(stage, c, up).wait_send()
         for j in range(3):
             for b in range(batches):
                 rs_copy(c, j, b).wait_send()
@@ -563,6 +619,7 @@
     for k in (1, 2, 3):
         xt_copy(k).wait_send()
         gz_copy(k).wait_send()
+        gy_copy(k).wait_send()
     for x_ in range(NX):
 
         @pl.when(jnp.logical_not(jnp.logical_and(home, x == x_)))
@@ -570,8 +627,9 @@
             gx_copy(x_).wait_send()
 
     for k in range(4):
-        copy(gz.at[4], gx.at[k], gx_s.at[0], gx_r.at[k], at(core_=other)).wait_recv()
-    gg_ref[...] = ((gx[0] + gx[1]) + (gx[2] + gx[3]))[:1]
+        copy(gy.at[4], gx.at[k], gx_s.at[0], gx_r.at[k], at(core_=other)).wait_recv()
+    total = (gx[0] + gx[1]) + (gx[2] + gx[3])
+    gg_ref[...] = jnp.concatenate([total[i : i + 1] for i in range(feats // 128)], axis=1)
 
 
 def per_device(states, gain, kv_weight, queries, out_grad, src_len):
@@ -598,6 +656,9 @@
             pltpu.VMEM((batches, tgt, heads_cols), BF16),
             pltpu.VMEM((batches, tgt, heads_cols), BF16),
             pltpu.VMEM((4, CHUNKS, feats, cols), BF16),
+            pltpu.VMEM((2, CHUNKS, feats, cols), BF16),
+            pltpu.VMEM((2, CHUNKS, feats // 2, cols), BF16),
+            pltpu.VMEM((4, cols, feats), BF16),
             pltpu.VMEM((2, 4, rows + 16, feats), BF16),
             pltpu.VMEM((4, 4, rows, feats), BF16),
             pltpu.VMEM((CHUNKS, rows, cols), F32),
@@ -617,13 +678,14 @@
             pltpu.VMEM((rows, 128), F32),
             pltpu.VMEM((16, 8, rows), F32),
             pltpu.VMEM((4, 8, rows), F32),
-            pltpu.VMEM((5, 8, feats), F32),
-            pltpu.VMEM((4, 8, feats), F32),
+            pltpu.VMEM((5, 4, 8, 128), F32),
+            pltpu.VMEM((5, 8, 128), F32),
+            pltpu.VMEM((4, 8, 128), F32),
             pltpu.VMEM((rows, 128), F32),
             pltpu.VMEM((2, rows, 128), F32),
             pltpu.VMEM((rows, 128), F32),
             dma((4,)),
-            dma((2, CHUNKS)), dma((2, CHUNKS)), dma((2, CHUNKS)), dma((2, CHUNKS)),
+            dma((5, 2, CHUNKS)), dma((5, 2, CHUNKS)),
             dma((2,)), dma((2,)),
             dma((2, 2)), dma((2, 2)), dma((2, 2)), dma((2, 2)),
             dma((2, 4)), dma((2, 4)),
@@ -634,6 +696,7 @@
             dma((2, 2, 3)), dma((2, 2, 3)),
             dma((2, 2)), dma((2, 2)),
             dma((16,)), dma((16,)),
+            dma((3,)), dma((3,)),
             dma((3,)), dma((3,)),
             dma((3,)), dma((3,)),
             dma((4,)), dma((4,)),

time: 165 us -> 149 us (0.903)
  Pallas kernels: 156 us -> 139 us
    pallas_call x1, Pallas kernels: 156 us -> 139 us  [per_device(): pl.pallas_call(kernel, out_shape=(jax.ShapeDtypeStruct((batches, tgt, hea...]
where the time goes in v3:
time: 149 us; the launch traced here: 148 us
  Pallas kernels  139 us (93%)
  local copies, waits for them, and re-layouts  6.74 us (5%)
    pallas_call x1, Pallas kernels, per_device(): pl.pallas_call(kernel, out_shape=(jax.ShapeDtypeStruct((batches, tgt, hea...  139 us
    unnamed x9, local copies, waits for them, and re-layouts  6.73 us

profile of v3, /device:TPU:1, one launch (start us, length us, event | category | flops | bytes accessed | tf_op | source)
XLA Modules:
  0.0 147.6 jit_solution(1473917294562712568)
XLA Ops:
  0.6 0.0 copy-start.1
  0.6 0.7 copy-done.1
  1.3 1.0 pad_maximum_fusion.ext_ref
  2.3 2.4 %copy.10 = bf16[64,8,2,512]{3,1,2,0:T(8,128)(2,1)} copy(bf16[64,8,2,512]{3,2,1,0:T(2,128)(2,1)} %bitcast.15) | data formatting | bytes 2097152
  4.7 0.0 copy-start
  4.7 0.7 copy-done
  5.4 139.2 %cross_attention.1 = (bf16[2,256,512]{2,1,0:T(8,128)(2,1)S(1)}, bf16[2,256,512]{2,1,0:T(8,128)(2,1)S(1)}, f32[256,512]{1,0:T(8,128)S(1)}, f32[1,512]{1,0:T(1,128)S(1)}) custom-call(bf16[512,1024]{1,0:T(8,128)(2,1)} %bitcast.14, bf16[272,512]{1,0:T(8,128)(2,1)S(1)} %pad_maximum_fusion.ext_ref, bf16[2,256,512]{2,1,0:T(8,128)(2,1)} %bitcast.16, ...), custom_call_target="tpu_custom_call" | custom-call | tf_op jit(solution)/shard_map/cross_attention/pallas_call | solution.py:644
  144.6 0.8 copy.15
  145.4 0.8 copy.16
  146.2 0.8 copy.17
  147.0 0.6 copy.18
  (1 shorter events, 0.0 us)
Async XLA Ops:
  0.6 0.7 copy-start.1
  4.7 0.7 copy-start

commit v4 on v3

--- a/solution.py
+++ b/solution.py
@@ -19,9 +19,9 @@
 
 
 def kernel(
-    w_ref, ext_ref, q_in, og_in, len_ref,
+    w_ref, states_in, gain_in, q_in, og_in, len_in,
     att_ref, gq_ref, gs_ref, gg_ref,
-    ext, q_ref, og_ref, wg, through, through_half, turned, raw, a, own_part, part_send, rs_recv, ag, dn, core_send, core_recv, z_send, z_recv, y_send, y_recv,
+    len_ref, ext, q_ref, og_ref, wg, through, through_half, turned, raw, a, own_part, part_send, rs_recv, ag, dn, core_send, core_recv, z_send, z_recv, y_send, y_recv,
     y_own, fin_send, fin, racc, small, xtot, gz, gy, gx, inv_ref, piece_inv, rsum_ref,
     local_sem, w_s, w_r, s1_s, s1_r, s2_s, s2_r, s2f_s, s2f_r, s3_s, s3_r, rs_s, rs_r, ag_s, ag_r,
     d1_s, d1_r, dz_s, dz_r, d2_s, d2_r, d3_s, d3_r, sm_s, sm_r, xt_s, xt_r, gz_s, gz_r, gy_s, gy_r, gx_s, gx_r,
@@ -47,10 +47,14 @@
     other = 1 - core
     home = t == x
 
-    load_ext = pltpu.make_async_copy(ext_ref, ext, local_sem.at[0])
+    load_ext = pltpu.make_async_copy(states_in, ext.at[:rows], local_sem.at[0])
+    load_gain = pltpu.make_async_copy(gain_in, ext.at[rows : rows + 16], local_sem.at[4])
+    load_len = pltpu.make_async_copy(len_in, len_ref, local_sem.at[5])
     load_q = pltpu.make_async_copy(q_in, q_ref, local_sem.at[1])
     load_og = pltpu.make_async_copy(og_in, og_ref, local_sem.at[2])
     load_ext.start()
+    load_gain.start()
+    load_len.start()
     load_q.start()
     load_og.start()
     barrier = pltpu.get_barrier_semaphore()
@@ -107,14 +111,14 @@
             (through_half.at[way, c], wg.at[2, c, part]),
             (through.at[way, c, rest], direct.at[rest]),
         )[stage]
-        return copy(here, there, w_s.at[stage, way, c], w_r.at[stage, way, c], above if up else below)
+        return copy(here, there, w_s.at[stage], w_r.at[stage, way, c], above if up else below)
 
     def w_send(c):
         for up in (True, False):
             for here, there in w_lanes(c):
                 copy(
                     w_ref.at[:, here], through.at[int(up), c, :, there],
-                    w_s.at[0, int(up), c], w_r.at[0, int(up), c], above if up else below,
+                    w_s.at[0], w_r.at[0, int(up), c], above if up else below,
                 ).start()
 
     def hop(stage, c):
@@ -125,6 +129,7 @@
                 w_copy(4, c, up).start()
 
     load_ext.wait()
+    load_gain.wait()
 
     def s1_copy(z, to):
         return copy(ext, raw.at[x // 2, y], s1_s.at[z], s1_r.at[x // 2], to)
@@ -196,30 +201,30 @@
     def s2_direct(half, up):
         to = at(y_=rotate(y, 1 if up else 3, NY))
         piece = raw.at[half, y]
-        return copy(piece, piece, s2_s.at[half, int(up)], s2_r.at[half, int(up)], to)
+        return copy(piece, piece, s2_s.at[0], s2_r.at[half, int(up)], to)
 
     def s2_arrival(half, up):
         to = at(y_=rotate(y, 1 if up else 3, NY))
         piece = raw.at[half, rotate(y, 3 if up else 1, NY)]
-        return copy(piece, piece, s2_s.at[half, int(up)], s2_r.at[half, int(up)], to)
+        return copy(piece, piece, s2_s.at[0], s2_r.at[half, int(up)], to)
 
     def s2_forward(half, up):
         to = at(y_=rotate(y, 1 if up else 3, NY))
         piece = raw.at[half, rotate(y, 3 if up else 1, NY), parts[0 if up else 1]]
-        return copy(piece, piece, s2f_s.at[half, int(up)], s2f_r.at[half, int(up)], to)
+        return copy(piece, piece, s2f_s.at[0], s2f_r.at[half, int(up)], to)
 
     def s2_last(half, up):
         to = at(y_=rotate(y, 1 if up else 3, NY))
         piece = raw.at[half, rotate(y, 2, NY), parts[0 if up else 1]]
-        return copy(piece, piece, s2f_s.at[half, int(up)], s2f_r.at[half, int(up)], to)
+        return copy(piece, piece, s2f_s.at[0], s2f_r.at[half, int(up)], to)
 
     def s3_copy(half, k):
         piece = a.at[core + 2 * half, rotate(y, 4 - k, NY)]
-        return copy(piece, piece, s3_s.at[half, k], s3_r.at[half, k], at(core_=other))
-
-    def s3_arrival(half, k):
-        piece = a.at[other + 2 * half, rotate(y, 4 - k, NY)]
-        return copy(piece, piece, s3_s.at[half, k], s3_r.at[half, k], at(core_=other))
+        return copy(piece, piece, s3_s.at[0], s3_r.at[0], at(core_=other))
+
+    def s3_all():
+        pieces = a.at[pl.ds(0, 2)]
+        return copy(pieces, pieces, s3_s.at[0], s3_r.at[0], at(core_=other))
 
     def normalise(half, k):
         s = rotate(y, 4 - k, NY)
@@ -278,12 +283,11 @@
             s2_last(half, up).wait_recv()
         normalise(half, 2)
     hop(2, 0)
+    load_len.wait()
     load_q.wait()
     load_og.wait()
     pltpu.make_async_copy(wg.at[0], wg.at[0], local_sem.at[3]).wait()
-    for half in (0, 1):
-        for k in (0, 1, 3, 2):
-            s3_arrival(half, k).wait_recv()
+    s3_all().wait_recv()
     hop(0, 2)
     hop(2, 1)
 
@@ -293,17 +297,21 @@
     def rs_copy(c, j, b):
         part = sequence(b)
         return copy(
-            part_send.at[c, j, part], rs_recv.at[c, j, part], rs_s.at[c, j, b], rs_r.at[c, j, b],
+            part_send.at[c, j, part], rs_recv.at[c, j, part], rs_s.at[0], rs_r.at[c, b],
             at(x_=rotate(x, 1 + j, NX)),
         )
 
+    def rs_arrived(c, b):
+        pieces = rs_recv.at[c, :, sequence(b)]
+        copy(pieces, pieces, rs_s.at[0], rs_r.at[c, b], at(core_=other)).wait_recv()
+
     def ag_copy(c, j, b):
         piece = ag.at[c, x, sequence(b)]
-        return copy(piece, piece, ag_s.at[c, j, b], ag_r.at[c, j, b], at(x_=rotate(x, 1 + j, NX)))
-
-    def ag_arrival(c, j, b):
-        piece = ag.at[c, rotate(x, 3 - j, NX), sequence(b)]
-        return copy(piece, piece, ag_s.at[c, j, b], ag_r.at[c, j, b], at(x_=rotate(x, 1 + j, NX)))
+        return copy(piece, piece, ag_s.at[0], ag_r.at[c, b], at(x_=rotate(x, 1 + j, NX)))
+
+    def ag_arrived(c, b):
+        pieces = ag.at[c, pl.ds(0, 3), sequence(b)]
+        copy(pieces, pieces, ag_s.at[0], ag_r.at[c, b], at(core_=other)).wait_recv()
 
     def project(c):
         for up in (True, False):
@@ -348,8 +356,8 @@
         def one(b, carry):
             at_rows = sequence(b)
             kv_b = own_part[c, at_rows, :]
+            rs_arrived(c, b)
             for j in range(3):
-                rs_copy(c, j, b).wait_recv()
                 kv_b = kv_b + rs_recv[c, j, at_rows, :].astype(F32)
             keys = two_heads(kv_b[:, :128].astype(BF16).astype(F32))
             values = two_heads(kv_b[:, 128:].astype(BF16).astype(F32))
@@ -379,9 +387,8 @@
 
     def back(chunks):
         for c in chunks:
-            for j in range(3):
-                for b in range(batches):
-                    ag_arrival(c, j, b).wait_recv()
+            for b in range(batches):
+                ag_arrived(c, b)
 
         def one(r, carry):
             term = dot_t(ag[chunks[0]].reshape(4 * rows, cols), wg[r, chunks[0]])
@@ -415,21 +422,27 @@
     for r in range(4):
         turned[r] = wg[r, last].T
     back((2,))
-    reduce_zl(8)
 
     def d1_copy(b, half, k):
         part = sequence(b)
         return copy(
             core_send.at[half, k, part], core_recv.at[half, k, part],
-            d1_s.at[b, half, k], d1_r.at[b, half, k], at(core_=other),
+            d1_s.at[0], d1_r.at[b, half, k], at(core_=other),
         )
 
+    SLOT = {1: 0, 3: 1, 2: 2}
+
     def d2_copy(b, half, k):
-        part = sequence(b)
+        part, slot, two = sequence(b), SLOT[k], int(k == 2)
         return copy(
-            y_send.at[half, k - 1, part], y_recv.at[half, k - 1, part],
-            d2_s.at[b, half, k - 1], d2_r.at[b, half, k - 1], at(y_=rotate(y, k, NY)),
+            y_send.at[half, slot, part], y_recv.at[half, slot, part], d2_s.at[two], d2_r.at[two, b],
+            at(y_=rotate(y, k, NY)),
         )
+
+    def d2_arrived(b):
+        pieces = y_recv.at[:, pl.ds(0, 2), sequence(b)]
+        copy(pieces, pieces, d2_s.at[0], d2_r.at[0, b], at(core_=other)).wait_recv()
+        d2_copy(b, 0, 2).wait_recv()
 
     def whole(b, xs, k):
         part = sequence(b)
@@ -446,35 +459,34 @@
         return v + core_recv[half, k, sequence(b), :].astype(F32)
 
     def cores(b):
-        for j in range(3):
-            ag_arrival(last, j, b).wait_recv()
+        ag_arrived(last, b)
         part = sequence(b)
         for k in (2, 1, 3, 0):
             for half in (0, 1):
                 core_send[half, k, part, :] = whole(b, other + 2 * half, k).astype(BF16)
                 d1_copy(b, half, k).start()
-        if b == 0:
-            reduce_y(8)
         z_send[part, :] = chip_sum(b, 1 - zl, 2).astype(BF16)
         dz_copy(b).start()
 
     def one_step(b):
         for half in (0, 1):
             for k in (1, 3):
-                y_send[half, k - 1, sequence(b), :] = chip_sum(b, half, k).astype(BF16)
+                y_send[half, SLOT[k], sequence(b), :] = chip_sum(b, half, k).astype(BF16)
                 d2_copy(b, half, k).start()
 
     def two_steps(b):
         part = sequence(b)
         v = chip_sum(b, zl, 2)
         dz_copy(b).wait_recv()
-        y_send[0, 1, part, :] = (v + z_recv[part, :].astype(F32)).astype(BF16)
+        y_send[0, 2, part, :] = (v + z_recv[part, :].astype(F32)).astype(BF16)
         d2_copy(b, 0, 2).start()
 
     cores(0)
     one_step(0)
+    reduce_zl(8)
     cores(1)
     two_steps(0)
+    reduce_y(8)
     one_step(1)
     two_steps(1)
     for b in range(batches):
@@ -491,15 +503,12 @@
 
     def deliver(b):
         part = pl.ds(b * src, src)
-        for k in (1, 3):
-            for half in (0, 1):
-                d2_copy(b, half, k).wait_recv()
-        d2_copy(b, 0, 2).wait_recv()
+        d2_arrived(b)
         for half in (0, 1):
             v = y_own[half, part, :]
             for k in (1, 3):
-                v = v + y_recv[half, k - 1, part, :].astype(F32)
-            v = v + jnp.where(zl == half, y_recv[0, 1, part, :].astype(F32), 0.0)
+                v = v + y_recv[half, SLOT[k], part, :].astype(F32)
+            v = v + jnp.where(zl == half, y_recv[0, 2, part, :].astype(F32), 0.0)
             fin_send[half, part, :] = v.astype(BF16)
 
             @pl.when(stays(half))
@@ -538,8 +547,8 @@
 
     gz[zh, 0] = folded(weighed(y_own[0], 0, 0) + weighed(y_own[1], 1, 0))
     for k in (1, 3):
-        gz[zh, k] = folded(weighed(y_send[0, k - 1], 0, k) + weighed(y_send[1, k - 1], 1, k))
-    gz[zh, 2] = folded(weighed(y_send[0, 1], zl, 2))
+        gz[zh, k] = folded(weighed(y_send[0, SLOT[k]], 0, k) + weighed(y_send[1, SLOT[k]], 1, k))
+    gz[zh, 2] = folded(weighed(y_send[0, 2], zl, 2))
     for k in (1, 2, 3):
         gz_copy(k).start()
     deliver(0)
@@ -552,6 +561,25 @@
     for k in (1, 2, 3):
         gy_copy(k).start()
 
+    def all_sent(pieces, sem, arrived):
+        copy(pieces, pieces, sem, arrived, at(core_=other)).wait_send()
+
+    all_sent(through, w_s.at[0], w_r.at[0, 0, 0])
+    for stage in range(1, 5):
+        all_sent(through_half, w_s.at[stage], w_r.at[stage, 0, 0])
+    all_sent(part_send, rs_s.at[0], rs_r.at[0, 0])
+    all_sent(ag.at[:, pl.ds(0, 3)], ag_s.at[0], ag_r.at[0, 0])
+    all_sent(raw.at[0], s2_s.at[0], s2_r.at[0, 0])
+    all_sent(raw.at[0, pl.ds(0, 2)], s2f_s.at[0], s2f_r.at[0, 0])
+    s3_all().wait_send()
+    all_sent(core_send, d1_s.at[0], d1_r.at[0, 0, 0])
+
+    @pl.when(jnp.logical_not(home))
+    def _():
+        s1_near.wait_send()
+
+    for k in (1, 2, 3):
+        xt_copy(k).wait_send()
     deliver(1)
 
     def owned(b):
@@ -582,42 +610,17 @@
     owned(0)
     owned(1)
 
-    def sent_w(c, carry):
-        for up in (True, False):
-            for stage in range(5):
-                w_copy(stage, c, up).wait_send()
-        for j in range(3):
-            for b in range(batches):
-                rs_copy(c, j, b).wait_send()
-                ag_copy(c, j, b).wait_send()
-        return carry
-
-    lax.fori_loop(0, CHUNKS, sent_w, 0)
-
-    @pl.when(jnp.logical_not(home))
-    def _():
-        s1_near.wait_send()
-
-    for half in (0, 1):
-        for up in (True, False):
-            s2_direct(half, up).wait_send()
-            s2_forward(half, up).wait_send()
-        for k in range(4):
-            s3_copy(half, k).wait_send()
-        for b in range(batches):
-            for k in range(4):
-                d1_copy(b, half, k).wait_send()
-            for k in (1, 3) if half else (1, 2, 3):
-                d2_copy(b, half, k).wait_send()
-            if half == 0:
-                dz_copy(b).wait_send()
+    all_sent(y_send.at[:, pl.ds(0, 2)], d2_s.at[0], d2_r.at[0, 0])
+    all_sent(y_send.at[0, 2], d2_s.at[1], d2_r.at[1, 0])
+    for b in range(batches):
+        dz_copy(b).wait_send()
+        for half in (0, 1):
 
             @pl.when(jnp.logical_not(stays(half)))
             def _():
                 d3_copy(b, half).wait_send()
 
     for k in (1, 2, 3):
-        xt_copy(k).wait_send()
         gz_copy(k).wait_send()
         gy_copy(k).wait_send()
     for x_ in range(NX):
@@ -638,7 +641,7 @@
     rows = batches * src
     cols = 2 * heads_cols // CHUNKS
     w = kv_weight.reshape(feats, 2 * heads_cols)
-    ext = jnp.concatenate([states.reshape(rows, feats), jnp.broadcast_to(gain[None, :], (16, feats))], axis=0)
+    gains = jnp.broadcast_to(gain[None, :], (16, feats))
     vmem = pl.BlockSpec(memory_space=pltpu.VMEM)
     dma = pltpu.SemaphoreType.DMA
     out = pl.pallas_call(
@@ -649,9 +652,10 @@
             jax.ShapeDtypeStruct((rows, feats), F32),
             jax.ShapeDtypeStruct((1, feats), F32),
         ),
-        in_specs=[pl.BlockSpec(memory_space=pl.ANY)] * 4 + [pl.BlockSpec(memory_space=pltpu.SMEM)],
+        in_specs=[pl.BlockSpec(memory_space=pl.ANY)] * 6,
         out_specs=[vmem] * 4,
         scratch_shapes=[
+            pltpu.SMEM((batches,), jnp.int32),
             pltpu.VMEM((rows + 16, feats), BF16),
             pltpu.VMEM((batches, tgt, heads_cols), BF16),
             pltpu.VMEM((batches, tgt, heads_cols), BF16),
@@ -684,16 +688,16 @@
             pltpu.VMEM((rows, 128), F32),
             pltpu.VMEM((2, rows, 128), F32),
             pltpu.VMEM((rows, 128), F32),
-            dma((4,)),
-            dma((5, 2, CHUNKS)), dma((5, 2, CHUNKS)),
+            dma((6,)),
+            dma((5,)), dma((5, 2, CHUNKS)),
             dma((2,)), dma((2,)),
-            dma((2, 2)), dma((2, 2)), dma((2, 2)), dma((2, 2)),
-            dma((2, 4)), dma((2, 4)),
-            dma((CHUNKS, 3, 2)), dma((CHUNKS, 3, 2)),
-            dma((CHUNKS, 3, 2)), dma((CHUNKS, 3, 2)),
-            dma((2, 2, 4)), dma((2, 2, 4)),
+            dma((1,)), dma((2, 2)), dma((1,)), dma((2, 2)),
+            dma((1,)), dma((1,)),
+            dma((1,)), dma((CHUNKS, 2)),
+            dma((1,)), dma((CHUNKS, 2)),
+            dma((1,)), dma((2, 2, 4)),
             dma((2,)), dma((2,)),
-            dma((2, 2, 3)), dma((2, 2, 3)),
+            dma((2,)), dma((2, 2)),
             dma((2, 2)), dma((2, 2)),
             dma((16,)), dma((16,)),
             dma((3,)), dma((3,)),
@@ -706,7 +710,7 @@
         ),
         name="cross_attention",
     )(
-        w, ext, queries[0], out_grad[0], src_len
+        w, states.reshape(rows, feats), gains, queries[0], out_grad[0], src_len
     )
     attended, grad_q, grad_states, grad_gain = out
     return attended[None], grad_q[None], grad_states.reshape(batches, src, feats), grad_gain[0]

time: 149 us -> 146 us (0.980)
    unnamed x9 -> x11, local copies, waits for them, and re-layouts: 6.73 us -> 6.77 us
where the time goes in v4:
time: 146 us
  Pallas kernels  138 us (95%)
  local copies, waits for them, and re-layouts  6.78 us (5%)
    pallas_call x1, Pallas kernels, per_device(): pl.pallas_call(kernel, out_shape=(jax.ShapeDtypeStruct((batches, tgt, hea...  138 us
    unnamed x11, local copies, waits for them, and re-layouts  6.77 us

profile of v4, /device:TPU:1, one launch (start us, length us, event | category | flops | bytes accessed | tf_op | source)
XLA Modules:
  0.0 145.6 jit_solution(15774290533637546403)
XLA Ops:
  0.6 0.0 copy-start.2
  0.6 0.7 copy-done.2
  1.3 0.0 copy-start
  1.3 2.5 %copy.10 = bf16[64,8,2,512]{3,1,2,0:T(8,128)(2,1)} copy(bf16[64,8,2,512]{3,2,1,0:T(2,128)(2,1)} %bitcast.16) | data formatting | bytes 2097152
  3.8 0.0 copy-start.1
  3.8 0.0 copy-done
  3.8 0.7 copy-done.1
  4.5 138.1 %cross_attention.1 = (bf16[2,256,512]{2,1,0:T(8,128)(2,1)S(1)}, bf16[2,256,512]{2,1,0:T(8,128)(2,1)S(1)}, f32[256,512]{1,0:T(8,128)S(1)}, f32[1,512]{1,0:T(1,128)S(1)}) custom-call(bf16[512,1024]{1,0:T(8,128)(2,1)} %bitcast.15, bf16[256,512]{1,0:T(8,128)(2,1)S(1)} %bitcast.13, bf16[16,512]{1,0:T(8,128)(2,1)S(1)} %broadcast_in_dim.12.gain_in, ...), custom_call_target="tpu_custom_call" | custom-call | tf_op jit(solution)/shard_map/cross_attention/pallas_call | solution.py:647
  142.6 0.8 copy.15
  143.4 0.8 copy.16
  144.2 0.8 copy.17
  145.0 0.6 copy.18
  (1 shorter events, 0.0 us)
Async XLA Ops:
  0.6 0.7 copy-start.2
  1.3 2.5 %copy-start = (bf16[2,128,512]{2,1,0:T(8,128)(2,1)S(1)}, bf16[2,128,512]{2,1,0:T(8,128)(2,1)}, u32[]{:S(2)}) copy-start(bf16[2,128,512]{2,1,0:T(8,128)(2,1)} %param.6) | copy-start | bytes 786436
  3.8 0.7 copy-start.1

commit v5 on v4

--- a/solution.py
+++ b/solution.py
@@ -113,13 +113,23 @@
         )[stage]
         return copy(here, there, w_s.at[stage], w_r.at[stage, way, c], above if up else below)
 
+    def w_send_way(c, up):
+        for here, there in w_lanes(c):
+            copy(
+                w_ref.at[:, here], through.at[int(up), c, :, there],
+                w_s.at[0], w_r.at[0, int(up), c], above if up else below,
+            ).start()
+
     def w_send(c):
         for up in (True, False):
-            for here, there in w_lanes(c):
-                copy(
-                    w_ref.at[:, here], through.at[int(up), c, :, there],
-                    w_s.at[0], w_r.at[0, int(up), c], above if up else below,
-                ).start()
+            w_send_way(c, up)
+
+    def w_send_first(outward):
+        for up in (True, False):
+
+            @pl.when((zl == int(up)) if outward else (zl != int(up)))
+            def _():
+                w_send_way(0, up)
 
     def hop(stage, c):
         for up in (True, False):
@@ -147,6 +157,7 @@
     def _():
         s1_local.start()
 
+    w_send_first(True)
     for c in range(CHUNKS):
         for here, there in w_lanes(c):
             pltpu.make_async_copy(w_ref.at[:, here], wg.at[0, c, :, there], local_sem.at[3]).start()
@@ -248,7 +259,7 @@
 
     reduce_zl(0)
     s1_far.wait_send()
-    w_send(0)
+    w_send_first(False)
     reduce_y(0)
     for half in (0, 1):
         copy(ext, raw.at[half, y], s1_s.at[0], s1_r.at[half], at(core_=other)).wait_recv()
@@ -326,7 +337,7 @@
             return acc
 
         def sequences(b, carry):
-            for j in range(3):
+            for j in (1, 0, 2):
                 part_send[c, j, sequence(b), :] = one(j, b).astype(BF16)
                 rs_copy(c, j, b).start()
             own_part[c, sequence(b), :] = one(3, b)
@@ -377,7 +388,7 @@
                 [jnp.where(first, dkey[:src], dkey[src:]), jnp.where(first, dvalue[:src], dvalue[src:])], axis=1
             ).astype(BF16)
             ag[c, x, at_rows, :] = dkv
-            for j in range(3):
+            for j in (1, 0, 2):
                 ag_copy(c, j, b).start()
             product = dkv.astype(F32) * kv_b
             racc[at_rows, :] = racc[at_rows, :] + (product[:, :128] + product[:, 128:])
@@ -423,8 +434,13 @@
         turned[r] = wg[r, last].T
     back((2,))
 
+    SHARES = ((0, src), (src, src // 2), (src + src // 2, src - src // 2))
+
+    def share(b):
+        return pl.ds(*SHARES[b])
+
     def d1_copy(b, half, k):
-        part = sequence(b)
+        part = share(b)
         return copy(
             core_send.at[half, k, part], core_recv.at[half, k, part],
             d1_s.at[0], d1_r.at[b, half, k], at(core_=other),
@@ -433,34 +449,35 @@
     SLOT = {1: 0, 3: 1, 2: 2}
 
     def d2_copy(b, half, k):
-        part, slot, two = sequence(b), SLOT[k], int(k == 2)
+        part, slot, two = share(b), SLOT[k], int(k == 2)
         return copy(
             y_send.at[half, slot, part], y_recv.at[half, slot, part], d2_s.at[two], d2_r.at[two, b],
             at(y_=rotate(y, k, NY)),
         )
 
     def d2_arrived(b):
-        pieces = y_recv.at[:, pl.ds(0, 2), sequence(b)]
+        pieces = y_recv.at[:, pl.ds(0, 2), share(b)]
         copy(pieces, pieces, d2_s.at[0], d2_r.at[0, b], at(core_=other)).wait_recv()
         d2_copy(b, 0, 2).wait_recv()
 
     def whole(b, xs, k):
-        part = sequence(b)
+        part = share(b)
         r = lax.rem(y + k + NZ - zh, NZ)
         return dn[xs, r, part, :] + jnp.dot(ag[last, xs, part, :], turned[r], preferred_element_type=F32)
 
     def dz_copy(b):
-        part = sequence(b)
+        part = share(b)
         return copy(z_send.at[part], z_recv.at[part], dz_s.at[b], dz_r.at[b], at(zl_=1 - zl))
 
     def chip_sum(b, half, k):
         v = whole(b, core + 2 * half, k)
         d1_copy(b, half, k).wait_recv()
-        return v + core_recv[half, k, sequence(b), :].astype(F32)
+        return v + core_recv[half, k, share(b), :].astype(F32)
 
     def cores(b):
-        ag_arrived(last, b)
-        part = sequence(b)
+        if b < batches:
+            ag_arrived(last, b)
+        part = share(b)
         for k in (2, 1, 3, 0):
             for half in (0, 1):
                 core_send[half, k, part, :] = whole(b, other + 2 * half, k).astype(BF16)
@@ -471,11 +488,11 @@
     def one_step(b):
         for half in (0, 1):
             for k in (1, 3):
-                y_send[half, SLOT[k], sequence(b), :] = chip_sum(b, half, k).astype(BF16)
+                y_send[half, SLOT[k], share(b), :] = chip_sum(b, half, k).astype(BF16)
                 d2_copy(b, half, k).start()
 
     def two_steps(b):
-        part = sequence(b)
+        part = share(b)
         v = chip_sum(b, zl, 2)
         dz_copy(b).wait_recv()
         y_send[0, 2, part, :] = (v + z_recv[part, :].astype(F32)).astype(BF16)
@@ -488,13 +505,16 @@
     two_steps(0)
     reduce_y(8)
     one_step(1)
+    cores(2)
     two_steps(1)
-    for b in range(batches):
+    one_step(2)
+    two_steps(2)
+    for b in range(3):
         for half in (0, 1):
-            y_own[half, sequence(b), :] = chip_sum(b, half, 0)
+            y_own[half, share(b), :] = chip_sum(b, half, 0)
 
     def d3_copy(b, half):
-        part = pl.ds(b * src, src)
+        part = share(b)
         to = (y, zh * 4 + core + 2 * half, x)
         return copy(fin_send.at[half, part], fin.at[zl, part], d3_s.at[b, half], d3_r.at[b, zl], to)
 
@@ -502,7 +522,7 @@
         return jnp.logical_and(home, x // 2 == half)
 
     def deliver(b):
-        part = pl.ds(b * src, src)
+        part = share(b)
         d2_arrived(b)
         for half in (0, 1):
             v = y_own[half, part, :]
@@ -581,9 +601,10 @@
     for k in (1, 2, 3):
         xt_copy(k).wait_send()
     deliver(1)
+    deliver(2)
 
     def owned(b):
-        part = pl.ds(b * src, src)
+        part = share(b)
         for k in (0, 1):
             copy(fin_send.at[0, part], fin.at[k, part], d3_s.at[b, 0], d3_r.at[b, k], at(core_=other)).wait_recv()
         dnormed = fin[0, part, :].astype(F32) + fin[1, part, :].astype(F32)
@@ -609,10 +630,11 @@
 
     owned(0)
     owned(1)
+    owned(2)
 
     all_sent(y_send.at[:, pl.ds(0, 2)], d2_s.at[0], d2_r.at[0, 0])
     all_sent(y_send.at[0, 2], d2_s.at[1], d2_r.at[1, 0])
-    for b in range(batches):
+    for b in range(3):
         dz_copy(b).wait_send()
         for half in (0, 1):
 
@@ -695,10 +717,10 @@
             dma((1,)), dma((1,)),
             dma((1,)), dma((CHUNKS, 2)),
             dma((1,)), dma((CHUNKS, 2)),
-            dma((1,)), dma((2, 2, 4)),
-            dma((2,)), dma((2,)),
-            dma((2,)), dma((2, 2)),
-            dma((2, 2)), dma((2, 2)),
+            dma((1,)), dma((3, 2, 4)),
+            dma((3,)), dma((3,)),
+            dma((2,)), dma((2, 3)),
+            dma((3, 2)), dma((3, 2)),
             dma((16,)), dma((16,)),
             dma((3,)), dma((3,)),
             dma((3,)), dma((3,)),

time: 146 us -> 144 us (0.986)
  Pallas kernels: 138 us -> 136 us
    pallas_call x1, Pallas kernels: 138 us -> 136 us  [per_device(): pl.pallas_call(kernel, out_shape=(jax.ShapeDtypeStruct((batches, tgt, hea...]
where the time goes in v5:
time: 144 us; the launch traced here: 143 us
  Pallas kernels  136 us (94%)
  local copies, waits for them, and re-layouts  6.78 us (5%)
    pallas_call x1, Pallas kernels, per_device(): pl.pallas_call(kernel, out_shape=(jax.ShapeDtypeStruct((batches, tgt, hea...  136 us
    unnamed x11, local copies, waits for them, and re-layouts  6.77 us

profile of v5, /device:TPU:1, one launch (start us, length us, event | category | flops | bytes accessed | tf_op | source)
XLA Modules:
  0.0 143.0 jit_solution(13385322762634017486)
XLA Ops:
  0.6 0.0 copy-start.2
  0.6 0.7 copy-done.2
  1.3 0.0 copy-start
  1.3 2.5 %copy.10 = bf16[64,8,2,512]{3,1,2,0:T(8,128)(2,1)} copy(bf16[64,8,2,512]{3,2,1,0:T(2,128)(2,1)} %bitcast.16) | data formatting | bytes 2097152
  3.8 0.0 copy-start.1
  3.8 0.0 copy-done
  3.8 0.7 copy-done.1
  4.5 135.6 %cross_attention.1 = (bf16[2,256,512]{2,1,0:T(8,128)(2,1)S(1)}, bf16[2,256,512]{2,1,0:T(8,128)(2,1)S(1)}, f32[256,512]{1,0:T(8,128)S(1)}, f32[1,512]{1,0:T(1,128)S(1)}) custom-call(bf16[512,1024]{1,0:T(8,128)(2,1)} %bitcast.15, bf16[256,512]{1,0:T(8,128)(2,1)S(1)} %bitcast.13, bf16[16,512]{1,0:T(8,128)(2,1)S(1)} %broadcast_in_dim.12.gain_in, ...), custom_call_target="tpu_custom_call" | custom-call | tf_op jit(solution)/shard_map/cross_attention/pallas_call | solution.py:669
  140.1 0.8 copy.15
  140.9 0.8 copy.16
  141.7 0.8 copy.17
  142.5 0.6 copy.18
  (1 shorter events, 0.0 us)
Async XLA Ops:
  0.6 0.7 copy-start.2
  1.3 2.5 %copy-start = (bf16[2,128,512]{2,1,0:T(8,128)(2,1)S(1)}, bf16[2,128,512]{2,1,0:T(8,128)(2,1)}, u32[]{:S(2)}) copy-start(bf16[2,128,512]{2,1,0:T(8,128)(2,1)} %param.6) | copy-start | bytes 786436
  3.8 0.7 copy-start.1

commit v6 on v5

--- a/solution.py
+++ b/solution.py
@@ -439,26 +439,26 @@
     def share(b):
         return pl.ds(*SHARES[b])
 
-    def d1_copy(b, half, k):
+    def d1_copy(b, k):
         part = share(b)
         return copy(
-            core_send.at[half, k, part], core_recv.at[half, k, part],
-            d1_s.at[0], d1_r.at[b, half, k], at(core_=other),
+            core_send.at[k, :, part], core_recv.at[k, :, part], d1_s.at[0], d1_r.at[b, k], at(core_=other)
         )
 
     SLOT = {1: 0, 3: 1, 2: 2}
 
-    def d2_copy(b, half, k):
+    def d2_copy(b, k):
+        halves = 0 if k == 2 else slice(None)
         part, slot, two = share(b), SLOT[k], int(k == 2)
         return copy(
-            y_send.at[half, slot, part], y_recv.at[half, slot, part], d2_s.at[two], d2_r.at[two, b],
+            y_send.at[halves, slot, part], y_recv.at[halves, slot, part], d2_s.at[two], d2_r.at[two, b],
             at(y_=rotate(y, k, NY)),
         )
 
     def d2_arrived(b):
         pieces = y_recv.at[:, pl.ds(0, 2), share(b)]
         copy(pieces, pieces, d2_s.at[0], d2_r.at[0, b], at(core_=other)).wait_recv()
-        d2_copy(b, 0, 2).wait_recv()
+        d2_copy(b, 2).wait_recv()
 
     def whole(b, xs, k):
         part = share(b)
@@ -470,9 +470,7 @@
         return copy(z_send.at[part], z_recv.at[part], dz_s.at[b], dz_r.at[b], at(zl_=1 - zl))
 
     def chip_sum(b, half, k):
-        v = whole(b, core + 2 * half, k)
-        d1_copy(b, half, k).wait_recv()
-        return v + core_recv[half, k, share(b), :].astype(F32)
+        return whole(b, core + 2 * half, k) + core_recv[k, half, share(b), :].astype(F32)
 
     def cores(b):
         if b < batches:
@@ -480,23 +478,25 @@
         part = share(b)
         for k in (2, 1, 3, 0):
             for half in (0, 1):
-                core_send[half, k, part, :] = whole(b, other + 2 * half, k).astype(BF16)
-                d1_copy(b, half, k).start()
+                core_send[k, half, part, :] = whole(b, other + 2 * half, k).astype(BF16)
+            d1_copy(b, k).start()
+        d1_copy(b, 2).wait_recv()
         z_send[part, :] = chip_sum(b, 1 - zl, 2).astype(BF16)
         dz_copy(b).start()
 
     def one_step(b):
-        for half in (0, 1):
-            for k in (1, 3):
+        for k in (1, 3):
+            d1_copy(b, k).wait_recv()
+            for half in (0, 1):
                 y_send[half, SLOT[k], share(b), :] = chip_sum(b, half, k).astype(BF16)
-                d2_copy(b, half, k).start()
+            d2_copy(b, k).start()
 
     def two_steps(b):
         part = share(b)
         v = chip_sum(b, zl, 2)
         dz_copy(b).wait_recv()
         y_send[0, 2, part, :] = (v + z_recv[part, :].astype(F32)).astype(BF16)
-        d2_copy(b, 0, 2).start()
+        d2_copy(b, 2).start()
 
     cores(0)
     one_step(0)
@@ -510,6 +510,7 @@
     one_step(2)
     two_steps(2)
     for b in range(3):
+        d1_copy(b, 0).wait_recv()
         for half in (0, 1):
             y_own[half, share(b), :] = chip_sum(b, half, 0)
 
@@ -592,7 +593,7 @@
     all_sent(raw.at[0], s2_s.at[0], s2_r.at[0, 0])
     all_sent(raw.at[0, pl.ds(0, 2)], s2f_s.at[0], s2f_r.at[0, 0])
     s3_all().wait_send()
-    all_sent(core_send, d1_s.at[0], d1_r.at[0, 0, 0])
+    all_sent(core_send, d1_s.at[0], d1_r.at[0, 0])
 
     @pl.when(jnp.logical_not(home))
     def _():
@@ -692,8 +693,8 @@
             pltpu.VMEM((CHUNKS, 3, rows, cols), BF16),
             pltpu.VMEM((CHUNKS, 4, rows, cols), BF16),
             pltpu.VMEM((4, 4, rows, feats), F32),
-            pltpu.VMEM((2, 4, rows, feats), BF16),
-            pltpu.VMEM((2, 4, rows, feats), BF16),
+            pltpu.VMEM((4, 2, rows, feats), BF16),
+            pltpu.VMEM((4, 2, rows, feats), BF16),
             pltpu.VMEM((rows, feats), BF16),
             pltpu.VMEM((rows, feats), BF16),
             pltpu.VMEM((2, 3, rows, feats), BF16),
@@ -717,7 +718,7 @@
             dma((1,)), dma((1,)),
             dma((1,)), dma((CHUNKS, 2)),
             dma((1,)), dma((CHUNKS, 2)),
-            dma((1,)), dma((3, 2, 4)),
+            dma((1,)), dma((3, 4)),
             dma((3,)), dma((3,)),
             dma((2,)), dma((2, 3)),
             dma((3, 2)), dma((3, 2)),

time: 144 us -> 143 us (level)
  no operation moved by 1% of the time
where the time goes in v6:
time: 143 us
  Pallas kernels  136 us (95%)
  local copies, waits for them, and re-layouts  6.78 us (5%)
    pallas_call x1, Pallas kernels, per_device(): pl.pallas_call(kernel, out_shape=(jax.ShapeDtypeStruct((batches, tgt, hea...  136 us
    unnamed x11, local copies, waits for them, and re-layouts  6.77 us

profile of v6, /device:TPU:1, one launch (start us, length us, event | category | flops | bytes accessed | tf_op | source)
XLA Modules:
  0.0 142.9 jit_solution(2177637802816866322)
XLA Ops:
  0.6 0.0 copy-start.2
  0.6 0.7 copy-done.2
  1.3 0.0 copy-start
  1.3 2.5 %copy.10 = bf16[64,8,2,512]{3,1,2,0:T(8,128)(2,1)} copy(bf16[64,8,2,512]{3,2,1,0:T(2,128)(2,1)} %bitcast.16) | data formatting | bytes 2097152
  3.8 0.0 copy-start.1
  3.8 0.0 copy-done
  3.8 0.7 copy-done.1
  4.5 135.5 %cross_attention.1 = (bf16[2,256,512]{2,1,0:T(8,128)(2,1)S(1)}, bf16[2,256,512]{2,1,0:T(8,128)(2,1)S(1)}, f32[256,512]{1,0:T(8,128)S(1)}, f32[1,512]{1,0:T(1,128)S(1)}) custom-call(bf16[512,1024]{1,0:T(8,128)(2,1)} %bitcast.15, bf16[256,512]{1,0:T(8,128)(2,1)S(1)} %bitcast.13, bf16[16,512]{1,0:T(8,128)(2,1)S(1)} %broadcast_in_dim.12.gain_in, ...), custom_call_target="tpu_custom_call" | custom-call | tf_op jit(solution)/shard_map/cross_attention/pallas_call | solution.py:670
  140.0 0.8 copy.15
  140.8 0.8 copy.16
  141.6 0.8 copy.17
  142.4 0.6 copy.18
  (1 shorter events, 0.0 us)
Async XLA Ops:
  0.6 0.7 copy-start.2
  1.3 2.5 %copy-start = (bf16[2,128,512]{2,1,0:T(8,128)(2,1)S(1)}, bf16[2,128,512]{2,1,0:T(8,128)(2,1)}, u32[]{:S(2)}) copy-start(bf16[2,128,512]{2,1,0:T(8,128)(2,1)} %param.6) | copy-start | bytes 786436
  3.8 0.7 copy-start.1
